TPU v7x, 128 devices: a whole 4x4x4 slice. The times are simulated.
128 devices in a mesh: row: 8 (over z, core), col: 16 (over y, x).
Axes of the slice: x: 4, y: 4, z: 4, core: 2. Of those that a mesh axis runs over, the one named last changes fastest.
Arguments:
- densities: bfloat16 [128, 3, 256, 128], P(('row', 'col')), may hold values from -6 to 6
- positions: float32 [128, 3, 256], replicated, may hold values from -1 to 1
- areas: float32 [128, 256], replicated, may hold values from 0.15 to 0.6
- bases: bfloat16 [128, 32, 3, 256], P(('row', 'col')), may hold values from -0.21875 to 0.21875
- near_pairs: int32 [1920, 2], replicated, may hold values from 0 to 127, as said below
- far_pairs: int32 [768, 2], replicated, may hold values from 0 to 127
- couplings: bfloat16 [768, 1024], replicated, may hold values from -1 to 1
Outputs:
- potentials: bfloat16 [128, 3, 256, 128], P(('row', 'col'))
Inputs may be any that keep to these rules, and one draw needn't show every extreme that they name: `near_pairs`: cluster g is held by the device of mesh row (g) // 16 and mesh column (g) % 16. For each mesh row i and column j, at most 40 rows (t, s) have t held in mesh row i and s held in mesh column j, and some (i, j) has exactly 40.
All inputs are finite; a program needn't handle non-finite values.
Results may differ from a plain program's by a relative error of at most 0.005.
Values may be sent and summed in bfloat16 or wider, within the bound.
No kernel may reach another device: no remote copies, remote signals or barrier semaphores. Data moves between devices by JAX's collectives and lax.ppermute only.
A program may use at most 128 MiB of HBM per device.

v0:
```python
import jax
import jax.numpy as jnp
from jax import lax
from jax.sharding import PartitionSpec as P

CS = 256
LOADS = 128
RANK = 32


eps_square = 0.0004
lame_ratio = 1.8
kelvin_coef = 1.0 / (16.0 * 3.141592653589793 * 0.7)


def kelvin_tile(pos_target, wt_target, pos_source, wt_source):
    offset = pos_target[:, :, None] - pos_source[:, None, :]
    inverse = lax.rsqrt(jnp.sum(offset * offset, axis=0) + eps_square)
    cubed = inverse * inverse * inverse
    weight = kelvin_coef * wt_target[:, None] * wt_source[None, :]
    identity = jnp.eye(3, dtype=jnp.float32)
    blocks = (
        offset[:, None] * offset[None, :] * cubed
        + lame_ratio * identity[:, :, None, None] * inverse
    ) * weight
    panels = pos_target.shape[1]
    return jnp.transpose(blocks, (0, 2, 1, 3)).reshape(3 * panels, 3 * panels).astype(jnp.bfloat16)


def compact(mask):
    length = mask.shape[0]
    place = jnp.cumsum(mask.astype(jnp.int32)) - 1
    destination = jnp.where(mask, place, length)
    chosen = (
        jnp.full((length + 1,), length - 1, jnp.int32)
        .at[destination]
        .set(jnp.arange(length, dtype=jnp.int32))
    )
    return (chosen[:length], jnp.sum(mask.astype(jnp.int32)))


def near_apply(
    targets,
    sources,
    mask,
    positions,
    areas,
    source_flat,
    source_place,
    target_place,
    target_count,
    back_flat,
    back_count,
):
    chosen, live_count = compact(mask)
    width = source_flat.shape[1]
    loads = source_flat.shape[2]
    totals = (jnp.zeros((target_count, width, loads), jnp.float32),)
    totals = totals + (jnp.zeros((back_count, width, loads), jnp.float32),)

    def one_turn(turn, carried):
        carried = list(carried)
        for half in range(2):
            slot = 2 * turn + half
            picked = chosen[slot]
            target = targets[picked]
            source = sources[picked]
            live = jnp.where(slot < live_count, 1.0, 0.0).astype(jnp.float32)
            tile = kelvin_tile(positions[target], areas[target], positions[source], areas[source])
            forward = jnp.dot(
                tile, source_flat[source_place(source)], preferred_element_type=jnp.float32
            )
            carried[0] = carried[0].at[target_place(target)].add(forward * live)
            backward = lax.dot_general(
                tile,
                back_flat[target_place(target)],
                (((0,), (0,)), ((), ())),
                preferred_element_type=jnp.float32,
            )
            other = jnp.where(target != source, live, 0.0)
            carried[1] = carried[1].at[source_place(source)].add(backward * other)
        return tuple(carried)

    return lax.fori_loop(0, (live_count + 1) // 2, one_turn, totals)


def far_apply(heads, tails, blocks, mask, source_moms, source_place, target_place, target_count):
    gathered = source_moms[source_place(tails)]
    products = jnp.einsum("frq,fql->frl", blocks, gathered, preferred_element_type=jnp.float32)
    matches = target_place(heads)[None, :] == jnp.arange(target_count, dtype=jnp.int32)[:, None]
    onehot = jnp.where(matches & mask[None, :], 1.0, 0.0).astype(jnp.float32)
    return jnp.einsum("af,frl->arl", onehot, products, precision=lax.Precision.HIGHEST)


def local(densities, positions, areas, bases, near_pairs, far_pairs, couplings):
    held = densities.shape[0]
    width = 3 * CS
    col_count = lax.axis_size("col")
    row_index = lax.axis_index("row")
    col_index = lax.axis_index("col")
    flat = densities.reshape(held, width, LOADS)
    basis_flat = bases.reshape(held, RANK, width)
    moments = jnp.einsum(
        "crw,cwl->crl", basis_flat, flat, preferred_element_type=jnp.float32
    ).astype(jnp.bfloat16)
    column_dens, column_moms = (
        lax.all_gather(densities, "row", axis=0, tiled=True),
        lax.all_gather(moments, "row", axis=0, tiled=True),
    )
    column_flat = column_dens.reshape(-1, width, LOADS)
    column_total = column_flat.shape[0]
    block_rows = col_count * held
    row_start = row_index * block_rows

    def row_place(cluster):
        return cluster - row_start

    def column_place(cluster):
        return cluster // held // col_count * held + cluster % held

    def in_row(cluster):
        return cluster // block_rows == row_index

    def in_column(cluster):
        return cluster // held % col_count == col_index

    heads = near_pairs[:, 0]
    tails = near_pairs[:, 1]
    far_heads = far_pairs[:, 0]
    far_tails = far_pairs[:, 1]
    blocks = couplings.reshape(-1, RANK, RANK)
    flipped = jnp.swapaxes(blocks, 1, 2)
    distinct_far = far_heads != far_tails
    no_slot = jnp.zeros((1,), bool)
    pad_row = jnp.reshape(row_start, (1,))
    pad_column = jnp.reshape(col_index * held, (1,))
    row_dens, row_moms = (
        lax.all_gather(densities, "col", axis=0, tiled=True),
        lax.all_gather(moments, "col", axis=0, tiled=True),
    )
    row_flat = row_dens.reshape(-1, width, LOADS)
    targets = jnp.concatenate([heads, pad_row])
    sources = jnp.concatenate([tails, pad_column])
    mask = jnp.concatenate([in_row(heads) & in_column(tails), no_slot])
    near_row, near_column = near_apply(
        targets,
        sources,
        mask,
        positions,
        areas,
        column_flat,
        column_place,
        row_place,
        block_rows,
        row_flat,
        column_total,
    )
    far_mask = in_row(far_heads) & in_column(far_tails)
    coef_row = far_apply(
        far_heads, far_tails, blocks, far_mask, column_moms, column_place, row_place, block_rows
    )
    coef_column = far_apply(
        far_tails,
        far_heads,
        flipped,
        far_mask & distinct_far,
        row_moms,
        row_place,
        column_place,
        column_total,
    )
    part_row, sum_row = (
        lax.psum_scatter(near_row, "col", scatter_dimension=0, tiled=True),
        lax.psum_scatter(coef_row, "col", scatter_dimension=0, tiled=True),
    )
    part_column, sum_column = (
        lax.psum_scatter(near_column, "row", scatter_dimension=0, tiled=True),
        lax.psum_scatter(coef_column, "row", scatter_dimension=0, tiled=True),
    )
    near_total = part_row + part_column
    coef_total = sum_row + sum_column
    expanded = jnp.einsum(
        "crw,crl->cwl", basis_flat.astype(jnp.float32), coef_total, precision=lax.Precision.HIGHEST
    )
    return (near_total + expanded).reshape(densities.shape).astype(jnp.bfloat16)


def solution(mesh):
    return jax.shard_map(
        local,
        mesh=mesh,
        in_specs=(
            P(("row", "col"), None, None, None),
            P(),
            P(),
            P(("row", "col"), None, None, None),
            P(),
            P(),
            P(),
        ),
        out_specs=P(("row", "col"), None, None, None),
        check_vma=False,
    )
```

profile of v0, /device:TPU:1, one launch (start us, length us, event | category | flops | bytes accessed | tf_op | source)
XLA Modules:
  0.0 1149.0 jit_solution(8192585258603077604)
XLA Ops:
  8.1 1.7 copy.26
  9.8 9.8 copy.30
  19.8 20.6 %all-gather.1 = bf16[512,128]{1,0:T(8,128)(2,1)S(1)} all-gather(bf16[32,128]{1,0:T(8,128)(2,1)S(1)} %fusion.43), channel_id=3, replica_groups=mesh['row'=8,'col'=16] {'col'}, dimensions={0}, use_global_device_ids=true | all-gather | bytes 139264 | tf_op jit(solution)/shard_map/all_gather | solution.py:139
  40.5 4.6 gather_fusion.1
  45.1 6.5 convolution_bitcast_fusion
  51.6 13.0 %fusion.37 = f32[8,32,128]{2,0,1:T(8,128)S(1)} fusion(f32[768,32,128]{2,1,0:T(8,128)S(1)} %convolution_bitcast_fusion, s32[768]{0:T(1024)S(1)} %get-tuple-element.367, pred[768]{0:T(1024)(128)(4,1)S(1)} %get-tuple-element.334), kind=kOutput, calls=%fused_computation.79 | convolution fusion | flops 302008320 | bytes 12717824 | tf_op jit(solution)/shard_map/af,frl->arl/dot_general | solution.py:92
  65.4 18.5 %all-gather = bf16[256,128]{1,0:T(8,128)(2,1)S(1)} all-gather(bf16[32,128]{1,0:T(8,128)(2,1)S(1)} %fusion.43), channel_id=2, replica_groups=mesh['row'=8,'col'=16] {'row'}, dimensions={0}, use_global_device_ids=true | all-gather | bytes 73728 | tf_op jit(solution)/shard_map/all_gather | solution.py:108
  83.9 4.4 gather_fusion
  88.3 11.4 convolution_bitcast_fusion.1
  99.7 14.5 %fusion.39 = f32[16,32,128]{2,0,1:T(8,128)S(1)} fusion(f32[768,32,128]{2,1,0:T(8,128)} %convolution_bitcast_fusion.1, s32[768]{0:T(1024)S(1)} %get-tuple-element.368, pred[768]{0:T(1024)(128)(4,1)S(1)} %get-tuple-element.335), kind=kOutput, calls=%fused_computation.81 | convolution fusion | flops 604016640 | bytes 12848896 | tf_op jit(solution)/shard_map/af,frl->arl/dot_general | solution.py:92
  119.2 10.5 scatter_custom_fusion
  129.7 3.3 broadcast_in_dim.40
  133.1 2.0 broadcast_in_dim.41
  135.0 266.2 %while.19 = (s32[]{:T(128)}, f32[16,768,128]{2,1,0:T(8,128)}, f32[8,768,128]{2,1,0:T(8,128)}, s32[]{:T(128)}, s32[1921]{0:T(1024)}, /*index=5*/s32[1921]{0:T(102...) while((s32[]{:T(128)}, f32[16,768,128]{2,1,0:T(8,128)}, ...), condition=%wide.region_11.12_spmd, body=%wide.region_4.11_spmd.sunk | while | flops 614204032 | bytes 31020416 | solution.py:84
  152.4 4.6 multiply_convert_fusion.3
  163.9 3.2 fusion.132
  169.8 3.0 fusion.133
  173.6 3.0 fusion.130
  176.5 2.9 fusion.131
  196.9 4.6 multiply_convert_fusion.3
  208.4 3.1 fusion.132
  214.2 3.0 fusion.133
  218.0 3.0 fusion.130
  221.0 2.9 fusion.131
  241.2 4.6 multiply_convert_fusion.3
  252.7 3.1 fusion.132
  258.6 3.0 fusion.133
  262.3 3.0 fusion.130
  265.3 2.9 fusion.131
  285.5 4.6 multiply_convert_fusion.3
  297.1 3.1 fusion.132
  302.9 3.0 fusion.133
  306.6 3.0 fusion.130
  309.6 2.9 fusion.131
  329.8 4.6 multiply_convert_fusion.3
  341.3 3.2 fusion.132
  347.2 3.0 fusion.133
  350.9 3.0 fusion.130
  353.9 2.9 fusion.131
  374.3 4.6 multiply_convert_fusion.3
  385.8 3.1 fusion.132
  391.6 3.0 fusion.133
  395.3 3.0 fusion.130
  398.3 2.9 fusion.131
  401.2 3.6 copy.25
  404.8 6.5 copy.24
  412.3 641.8 %reduce-scatter.9.cloned.1.call-done = f32[1,768,128]{1,2,0:T(8,128)} async-done(((f32[8,768,128]{1,2,0:T(8,128)}), f32[1,768,128]{1,2,0:T(8,128)}) %reduce-scatter.9.cloned.1.call-update) | async-done | bytes 393232 | tf_op jit(solution)/shard_map/reduce_scatter | solution.py:177
  1054.1 85.3 %reduce-scatter.13.cloned.1.call-done = f32[1,768,128]{1,2,0:T(8,128)} async-done(((f32[16,768,128]{1,2,0:T(8,128)}), f32[1,768,128]{1,2,0:T(8,128)}) %reduce-scatter.13.cloned.1.call-update) | async-done | bytes 393232
  (193 shorter events, 61.9 us)
Async XLA Ops:
  6.5 123.2 %all-gather.5.cloned.1.call-start = ((), (), s32[]{:S(2)}) async-start(), calls=%async_computation.4 | async-start | bytes 1769472 | tf_op jit(solution)/shard_map/all_gather | solution.py:107
  7.3 122.5 %all-gather.7.cloned.1.call-start = ((), (), s32[]{:S(2)}) async-start(), calls=%async_computation.5 | async-start | bytes 3342336 | tf_op jit(solution)/shard_map/all_gather | solution.py:138
  8.0 404.2 %reduce-scatter.11.cloned.1.call-start = ((), (), s32[]{:S(2)}) async-start(), calls=%async_computation.7 | async-start | bytes 147456 | tf_op jit(solution)/shard_map/reduce_scatter | solution.py:178
  9.8 9.8 copy-start.1
  9.8 9.8 copy-start.3
  9.8 30.6 %copy-start.8 = (s32[768,2]{0,1:T(2,128)S(1)}, s32[768,2]{0,1:T(2,128)}, u32[]{:S(2)}) copy-start(s32[768,2]{0,1:T(2,128)} %param.22) | copy-start | bytes 18436
  65.4 346.9 %reduce-scatter.15.cloned.1.call-start = ((), (), s32[]{:S(2)}) async-start(), calls=%async_computation.9 | async-start | bytes 278528
  99.7 15.3 %copy-start.5 = (s32[1920,2]{0,1:T(2,128)S(1)}, s32[1920,2]{0,1:T(2,128)}, u32[]{:S(2)}) copy-start(s32[1920,2]{0,1:T(2,128)} %param.21) | copy-start | bytes 46084
  99.7 18.4 %copy-start.2 = (f32[128,3,256]{2,0,1:T(8,128)S(1)}, f32[128,3,256]{2,0,1:T(8,128)}, u32[]{:S(2)}) copy-start(f32[128,3,256]{2,0,1:T(8,128)} %param.18) | copy-start | bytes 1179652
  115.0 939.1 %reduce-scatter.9.cloned.1.call-start = ((), (), s32[]{:S(2)}) async-start(), calls=%async_computation.6 | async-start | bytes 3538944 | tf_op jit(solution)/shard_map/reduce_scatter | solution.py:177
  133.1 2.0 copy-start.6
  152.4 8.4 copy-start.7
  163.9 3.2 copy-start
  196.9 8.4 copy-start.7
  208.4 3.1 copy-start
  241.2 8.4 copy-start.7
  252.7 3.1 copy-start
  285.5 8.4 copy-start.7
  297.1 3.1 copy-start
  329.8 8.4 copy-start.7
  341.3 3.2 copy-start
  374.3 8.4 copy-start.7
  385.8 3.1 copy-start
  404.8 734.7 %reduce-scatter.13.cloned.1.call-start = ((), (), s32[]{:S(2)}) async-start(), calls=%async_computation.8 | async-start | bytes 6684672
  411.3 0.8 copy-start.4
Sparse Core Ops, SparseCore 0:
  9.0 28.1 all-gather.4
  39.4 47.1 all-gather.6
  89.0 27.0 reduce-scatter.10
  119.4 71.8 reduce-scatter.14
  404.9 649.1 reduce-scatter.8
  1057.4 82.0 reduce-scatter.12
where the time goes:
time: 1170 us; the launch traced here: 1150 us
  waiting for transfers between devices  729 us (62%)
  matrix products  119 us (10%)
  loops' own time  115 us (10%)
  local copies, waits for them, and re-layouts  76.8 us (7%)
  other arithmetic  55.9 us (5%)
  blocking collectives  39.1 us (3%)
  between operations  14.6 us (1%)
    reduce_scatter x1, waiting for transfers between devices, local(): lax.psum_scatter(near_column, 'row', scatter_dimension=0, tiled=True)  642 us
    another operation x1, loops' own time, near_apply(): return lax.fori_loop(0, (live_count + 1) // 2, one_turn, totals)  115 us
    unnamed x8, waiting for transfers between devices  86.8 us
    dot_general x12, matrix products, one_turn(): lax.dot_general(tile, back_flat[target_place(target)], (((0,), (0,)), (()...  36.8 us
    dot_general x12, matrix products, one_turn(): jnp.dot(tile, source_flat[source_place(source)], preferred_element_type=j...  35.1 us
    convert_element_type x6, other arithmetic, kelvin_tile(): jnp.transpose(blocks, (0, 2, 1, 3)).reshape(3 * panels, 3 * panels)  27.8 us
    dot_general x2, matrix products, far_apply(): jnp.einsum('af,frl->arl', onehot, products, precision=lax.Precision.HIGHEST)  27.5 us
  transfers between devices with their start and end apart: 6, of which 2 were waited for; matrix products, arithmetic and copies ran while one was open for 22% of the time, Pallas kernels for 0%

commit v1 on v0

v1 whole, which is shorter than its diff:
```python
import functools

import jax
import jax.numpy as jnp
from jax import lax
from jax.experimental import pallas as pl
from jax.experimental.pallas import tpu as pltpu
from jax.sharding import PartitionSpec as P


CS = 256
LOADS = 128
RANK = 32
HALF = CS // 2
DENS = 3 * HALF
UNIT = 2 * DENS + RANK
FULL = 3 * CS + RANK
AXES = ("row", "col")
SIDE = 4

eps_square = 0.0004
lame_ratio = 1.8
kelvin_coef = 1.0 / (16.0 * 3.141592653589793 * 0.7)
VMEM_LIMIT = 48 * 1024 * 1024
bf16 = jnp.bfloat16
f32 = jnp.float32


def routes(move):
    pairs = []
    for z in range(SIDE):
        for core in range(2):
            for y in range(SIDE):
                for x in range(SIDE):
                    to_z, to_core, to_y, to_x = move(z, core, y, x)
                    source = (z * 2 + core) * 16 + y * SIDE + x
                    target = ((to_z % SIDE) * 2 + to_core) * 16 + (to_y % SIDE) * SIDE + to_x % SIDE
                    pairs.append((source, target))
    return pairs


def swap_core(value):
    return lax.ppermute(value, AXES, routes(lambda z, c, y, x: (z, 1 - c, y, x)))


def along_first(value, step):
    move = lambda z, c, y, x: (z, c, y, x + step) if c == 0 else (z, c, y + step, x)
    return lax.ppermute(value, AXES, routes(move))


def along_second(value, step):
    move = lambda z, c, y, x: (z, c, y + step, x) if c == 0 else (z, c, y, x + step)
    return lax.ppermute(value, AXES, routes(move))


def along_z(value, step):
    return lax.ppermute(value, AXES, routes(lambda z, c, y, x: (z + step, c, y, x)))


def whole(count):
    return [pl.BlockSpec(memory_space=pltpu.VMEM)] * count


def dot32(a, b):
    return jnp.dot(a, b, preferred_element_type=f32)


def prepare_kernel(core_ref, dens_ref, bases_ref, own_ref, other_ref, moments_ref):
    core = core_ref[0]
    total = jnp.zeros((RANK, LOADS), f32)
    mine = pl.multiple_of(core * HALF, HALF)
    theirs = pl.multiple_of((1 - core) * HALF, HALF)
    for j in range(3):
        total += dot32(bases_ref[0, :, j, :], dens_ref[0, j])
        own_ref[j * HALF : (j + 1) * HALF] = dens_ref[0, j, pl.ds(mine, HALF), :]
        other_ref[j * HALF : (j + 1) * HALF] = dens_ref[0, j, pl.ds(theirs, HALF), :]
    moments_ref[...] = total.astype(bf16)


def prepare(core, densities, bases):
    half = jax.ShapeDtypeStruct((DENS, LOADS), bf16)
    return pl.pallas_call(
        prepare_kernel,
        out_shape=(half, half, jax.ShapeDtypeStruct((RANK, LOADS), bf16)),
        in_specs=[pl.BlockSpec(memory_space=pltpu.SMEM)] + whole(2),
        out_specs=tuple(whole(3)),
        name="moments_and_halves",
    )(jnp.reshape(core, (1,)), densities, bases)


def near_kernel(first_unit, buffers, is_first, is_last, counts, sources, targets, blocks, *refs):
    units = 2 * buffers
    slots = 2 * units
    held = refs[:buffers]
    refs = refs[buffers:]
    if not is_first:
        carried, refs = refs[0], refs[1:]
    if is_last:
        keep, send, refs = refs[0], refs[1], refs[2:]
    else:
        result, refs = refs[0], refs[1:]
    acc, flat, spread, tile, code, weight, sems = refs

    copies = []
    for k in range(buffers):
        place = flat.at[k * 2 * UNIT : (k + 1) * 2 * UNIT]
        copies.append(pltpu.make_async_copy(held[k], place, sems.at[k]))
        copies[-1].start()

    def list_target(t, filled):
        for s in range(slots):
            count = counts[t, 2 * first_unit + s]
            code[filled] = t * 64 + s
            weight[filled] = count
            filled = filled + jnp.where(count > 0, 1, 0)
        code[filled] = t * 64
        weight[filled] = 0
        return filled + (filled & 1)

    entries = lax.fori_loop(0, 8, list_target, 0)
    for t in range(8):
        columns = jnp.transpose(targets[t])
        for i in range(4):
            spread[t, i] = jnp.broadcast_to(columns[:, i : i + 1], (CS, HALF))
    if is_first:
        acc[:, : 3 * CS] = jnp.zeros((8, 3 * CS, LOADS), f32)
    else:
        acc[...] = carried[...]
    for copy in copies:
        copy.wait()

    moments = jnp.concatenate(
        [flat[u * UNIT + 2 * DENS : (u + 1) * UNIT, :] for u in range(units)], axis=0
    )
    far = dot32(blocks[...], moments)
    for t in range(8):
        part = far[t * RANK : (t + 1) * RANK]
        if is_first:
            acc[t, 3 * CS :] = part
        else:
            acc[t, 3 * CS :] += part

    def make_tile(t, slot, amount):
        rows = []
        for h in range(2):
            row = sources[2 * first_unit + slot[h]]
            rows.append((row[0:1], row[1:2], row[2:3], row[3:4] * amount[h]))
        step = 16
        for at in range(0, CS, step):
            here = [spread[t, i, at : at + step] for i in range(4)]
            for h in range(2):
                lanes = slice(h * HALF, (h + 1) * HALF)
                dx, dy, dz = (here[i] - rows[h][i] for i in range(3))
                inverse = lax.rsqrt(dx * dx + dy * dy + dz * dz + eps_square)
                scaled = (here[3] * rows[h][3]) * inverse
                cubed = scaled * (inverse * inverse)
                level = lame_ratio * scaled
                ex, ey, ez = dx * cubed, dy * cubed, dz * cubed
                values = (dx * ex + level, dy * ey + level, dz * ez + level, dx * ey, dx * ez, dy * ez)
                for b in range(6):
                    tile[b, at : at + step, lanes] = values[b].astype(bf16)

    def add_products(t, slot):
        f = []
        for j in range(3):
            parts = []
            for h in range(2):
                base = slot[h] // 2 * UNIT + slot[h] % 2 * DENS + j * HALF
                parts.append(flat[pl.ds(pl.multiple_of(base, 16), HALF), :])
            f.append(jnp.concatenate(parts, axis=0))
        xy = dot32(tile[3], jnp.concatenate([f[1], f[0]], axis=1))
        xz = dot32(tile[4], jnp.concatenate([f[2], f[0]], axis=1))
        yz = dot32(tile[5], jnp.concatenate([f[2], f[1]], axis=1))
        acc[t, :CS] += xy[:, :LOADS] + xz[:, :LOADS] + dot32(tile[0], f[0])
        acc[t, CS : 2 * CS] += xy[:, LOADS:] + yz[:, :LOADS] + dot32(tile[1], f[1])
        acc[t, 2 * CS : 3 * CS] += xz[:, LOADS:] + yz[:, LOADS:] + dot32(tile[2], f[2])

    def task(k, carry):
        t = code[2 * k] // 64
        slot = [code[2 * k + h] % 64 for h in range(2)]
        amount = [weight[2 * k + h].astype(f32) * kelvin_coef for h in range(2)]
        make_tile(t, slot, amount)
        add_products(t, slot)
        return carry

    lax.fori_loop(0, entries // 2, task, 0)
    if is_last:
        keep[...] = acc[:4]
        send[...] = acc[4:].astype(bf16)
    else:
        result[...] = acc[...]


def near(first_unit, buffers, carried, is_last, counts, sources, targets, blocks):
    count = len(buffers)
    slots = 4 * count
    is_first = carried is None
    if is_last:
        shapes = (
            jax.ShapeDtypeStruct((4, FULL, LOADS), f32),
            jax.ShapeDtypeStruct((4, FULL, LOADS), bf16),
        )
        out_specs = tuple(whole(2))
    else:
        shapes = jax.ShapeDtypeStruct((8, FULL, LOADS), f32)
        out_specs = whole(1)[0]
    operands = [counts, sources, targets, blocks] + list(buffers)
    specs = [pl.BlockSpec(memory_space=pltpu.SMEM)] + whole(3)
    specs += [pl.BlockSpec(memory_space=pl.ANY)] * count
    if not is_first:
        operands.append(carried)
        specs += whole(1)
    return pl.pallas_call(
        functools.partial(near_kernel, first_unit, count, is_first, is_last),
        out_shape=shapes,
        in_specs=specs,
        out_specs=out_specs,
        scratch_shapes=[
            pltpu.VMEM((8, FULL, LOADS), f32),
            pltpu.VMEM((count * 2 * UNIT, LOADS), bf16),
            pltpu.VMEM((8, 4, CS, HALF), f32),
            pltpu.VMEM((6, CS, CS), bf16),
            pltpu.SMEM((8 * slots + 16,), jnp.int32),
            pltpu.SMEM((8 * slots + 16,), jnp.int32),
            pltpu.SemaphoreType.DMA((count,)),
        ],
        compiler_params=pltpu.CompilerParams(vmem_limit_bytes=VMEM_LIMIT),
        cost_estimate=pl.CostEstimate(
            flops=count * 1_000_000_000, bytes_accessed=8_000_000, transcendentals=count * 500_000
        ),
        name=f"near_from_{first_unit}",
    )(*operands)


def finish_kernel(keep, swapped, one, two, three, bases, out):
    def total(rows):
        return (
            keep[rows] + swapped[rows].astype(f32) + one[rows].astype(f32)
            + two[rows].astype(f32) + three[rows].astype(f32)
        )

    coefficients = total(slice(3 * CS, FULL))
    high = coefficients.astype(bf16)
    low = (coefficients - high.astype(f32)).astype(bf16)
    both = jnp.concatenate([high, low], axis=0)
    for j in range(3):
        basis = bases[0, :, j, :]
        twice = jnp.concatenate([basis, basis], axis=0)
        expanded = lax.dot_general(
            twice, both, (((0,), (0,)), ((), ())), preferred_element_type=f32
        )
        out[0, j] = (total(slice(j * CS, (j + 1) * CS)) + expanded).astype(bf16)


def finish(keep, swapped, others, bases):
    return pl.pallas_call(
        finish_kernel,
        out_shape=jax.ShapeDtypeStruct((1, 3, CS, LOADS), bf16),
        in_specs=whole(6),
        out_specs=whole(1)[0],
        name="sum_and_expand",
    )(keep, swapped, *others, bases)


def local(densities, positions, areas, bases, near_pairs, far_pairs, couplings):
    row = lax.axis_index("row")
    col = lax.axis_index("col")
    z, core = row // 2, row % 2
    y, x = col // SIDE, col % SIDE
    first_at = jnp.where(core == 0, x, y)
    second_at = jnp.where(core == 0, y, x)

    def unit_of(cluster):
        on_y, on_x = cluster // SIDE % SIDE, cluster % SIDE
        first = (jnp.where(core == 0, on_x, on_y) - first_at) % SIDE
        second = (jnp.where(core == 0, on_y, on_x) - second_at) % SIDE
        put = lambda r: jnp.where(r == 0, 0, jnp.where(r == 1, 2, jnp.where(r == 2, 3, 1)))
        return put(second) * SIDE + put(first)

    def other_core(cluster):
        return (cluster // 16 % 2 + core) % 2

    def slot_of(cluster):
        return jnp.where(cluster // 32 == z, unit_of(cluster) * 2 + other_core(cluster), -1)

    def target_of(cluster):
        place = other_core(cluster) * 4 + (cluster // 32 - z) % SIDE
        return jnp.where(cluster % 16 == col, place, -1)

    own, other, moments = prepare(core, densities, bases)
    partner = swap_core(other)
    unit = jnp.concatenate([own, partner, moments], axis=0)
    from_below = along_first(unit, 1)
    from_above = along_first(unit, -1)
    from_across = along_first(unit, 2)

    heads, tails = near_pairs[:, 0], near_pairs[:, 1]
    mark = lambda index, size: index[None, :] == jnp.arange(size, dtype=jnp.int32)[:, None]
    to_targets = jnp.concatenate(
        [target_of(heads), jnp.where(heads != tails, target_of(tails), -1)]
    )
    from_slots = jnp.concatenate([slot_of(tails), slot_of(heads)])
    counts = lax.dot_general(
        mark(to_targets, 8).astype(bf16),
        mark(from_slots, 32).astype(bf16),
        (((1,), (1,)), ((), ())),
        preferred_element_type=f32,
    ).astype(jnp.int32)

    far_heads, far_tails = far_pairs[:, 0], far_pairs[:, 1]

    def cell(target, source):
        ours = (target_of(target) >= 0) & (slot_of(source) >= 0) & (other_core(source) == 0)
        return jnp.where(ours, target_of(target) * 16 + unit_of(source), -1)

    forward = dot32(mark(cell(far_heads, far_tails), 128).astype(bf16), couplings)
    back_cell = jnp.where(far_heads != far_tails, cell(far_tails, far_heads), -1)
    backward = dot32(mark(back_cell, 128).astype(bf16), couplings)
    forward = forward.reshape(8, 16, RANK, RANK)
    backward = backward.reshape(8, 16, RANK, RANK)
    blocks = jnp.transpose(forward, (0, 2, 1, 3)) + jnp.transpose(backward, (0, 3, 1, 2))
    blocks = blocks.reshape(8 * RANK, 16 * RANK).astype(bf16)

    table = jnp.concatenate([positions, areas[:, None, :]], axis=1)
    slots = jnp.arange(32, dtype=jnp.int32)
    undo = lambda o: (jnp.where(o == 0, 0, jnp.where(o == 1, 3, jnp.where(o == 2, 1, 2))))
    slot_first = (undo(slots // 2 % 4) + first_at) % SIDE
    slot_second = (undo(slots // 8) + second_at) % SIDE
    slot_y = jnp.where(core == 0, slot_second, slot_first)
    slot_x = jnp.where(core == 0, slot_first, slot_second)
    slot_cluster = (slots % 2 + core) % 2 * 16 + slot_y * SIDE + slot_x
    plane = lax.dynamic_slice(table, (z * 32, 0, core * HALF), (32, 4, HALF))
    sources = jnp.take(plane, slot_cluster, axis=0)
    places = jnp.arange(8, dtype=jnp.int32)
    place_row = (places % 4 + z) % SIDE * 2 + (places // 4 + core) % 2
    targets = jnp.take(table, place_row * 16 + col, axis=0)
    targets = jnp.concatenate([targets, jnp.zeros((8, 4, CS), f32)], axis=1)

    tables = (counts, sources, targets)
    low = jnp.concatenate([unit, from_below], axis=0)
    high = jnp.concatenate([from_above, from_across], axis=0)
    low_below = along_second(low, 1)
    high_above = along_second(high, -1)
    high_below = along_second(high, 1)
    low_above = along_second(low, -1)
    low_across = along_second(low_below, 1)
    high_across = along_second(high_above, -1)

    part = lambda a, b: blocks[:, a * RANK : b * RANK]
    acc = near(0, (low, high), None, False, *tables, part(0, 4))
    acc = near(4, (low_below, high_below, low_above, high_above), acc, False, *tables, part(4, 12))
    keep, send = near(12, (low_across, high_across), acc, True, *tables, part(12, 16))

    swapped = swap_core(send)
    both = [(keep[k] + swapped[k].astype(f32)).astype(bf16) for k in range(1, 4)]
    others = [along_z(both[k - 1], k) for k in range(1, 4)]
    return finish(keep[0], swapped[0], others, bases)


def solution(mesh):
    return jax.shard_map(
        local,
        mesh=mesh,
        in_specs=(
            P(("row", "col"), None, None, None),
            P(),
            P(),
            P(("row", "col"), None, None, None),
            P(),
            P(),
            P(),
        ),
        out_specs=P(("row", "col"), None, None, None),
        check_vma=False,
    )
```

time: 1170 us -> 101 us (0.09)
  the two profiles are of different devices: /device:TPU:1 before, /device:TPU:24 now
where the time goes in v1:
time: 101 us; the launch traced here: 100 us
  Pallas kernels  39 us (39%)
  waiting for transfers between devices  22.9 us (23%)
  local copies, waits for them, and re-layouts  16.9 us (17%)
  starting transfers between devices  14.7 us (15%)
  other arithmetic  5.28 us (5%)
    pallas_call x3, Pallas kernels, near(): pl.pallas_call(functools.partial(near_kernel, first_unit, count, is_first...  35 us
    ppermute x3, waiting for transfers between devices, along_z(): lax.ppermute(value, AXES, routes(lambda z, c, y, x: (z + step, c, y, x)))  9.4 us
    ppermute x3, waiting for transfers between devices, along_first(): return lax.ppermute(value, AXES, routes(move))  6.83 us
    ppermute x6, starting transfers between devices, along_second(): return lax.ppermute(value, AXES, routes(move))  6.69 us
    unnamed x27, local copies, waits for them, and re-layouts  5.96 us
    reshape x2, local copies, waits for them, and re-layouts, local(): backward = backward.reshape(8, 16, RANK, RANK)  5.04 us
    ppermute x3, starting transfers between devices, along_first(): return lax.ppermute(value, AXES, routes(move))  4.64 us
    ppermute x6, waiting for transfers between devices, along_second(): return lax.ppermute(value, AXES, routes(move))  4.31 us
  transfers between devices with their start and end apart: 14, of which 9 were waited for; matrix products, arithmetic and copies ran while one was open for 17% of the time, Pallas kernels for 24%

profile of v1, /device:TPU:24, one launch (start us, length us, event | category | flops | bytes accessed | tf_op | source)
XLA Modules:
  0.0 100.0 jit_solution(12833672301515434852)
XLA Ops:
  0.0 1.6 %copy.15.bases_ref.bases = bf16[1,32,3,256]{3,2,1,0:T(4,128)(2,1)} copy(bf16[1,32,3,256]{3,1,2,0:T(8,128)(2,1)} %param.10) | data formatting | bytes 98304 | tf_op args[3]
  1.6 1.7 %moments_and_halves.1 = (bf16[384,128]{1,0:T(8,128)(2,1)}, bf16[384,128]{1,0:T(8,128)(2,1)}, bf16[32,128]{1,0:T(8,128)(2,1)}) custom-call(s32[1]{0:T(128)} %bitcast.4.core_ref, bf16[1,3,256,128]{3,2,1,0:T(8,128)(2,1)} %dens_ref.1, bf16[1,32,3,256]{3,2,1,0:T(4,128)(2,1)} %copy.15.bases_ref.bases), custom_call_target="tpu_custom_call" | custom-call | tf_op jit(solution)/shard_map/moments_and_halves/pallas_call | solution.py:82
  3.4 0.8 slice_reduce_fusion.2
  4.3 0.4 fusion.2
  4.7 2.0 %reshape.858 = f32[8,16,32,32]{3,2,1,0:T(8,128)} reshape(f32[128,1024]{1,0:T(8,128)S(1)} %fusion.2) | data formatting | bytes 1048576 | tf_op jit(solution)/shard_map/reshape | solution.py:320
  6.7 3.0 %copy.14 = f32[8,16,32,32]{2,1,3,0:T(8,128)} copy(f32[8,16,32,32]{3,2,1,0:T(8,128)} %reshape.858) | data formatting | bytes 1048576 | tf_op jit(solution)/shard_map/reshape | solution.py:320
  9.7 0.4 fusion.1
  10.1 2.0 %reshape.857 = f32[8,16,32,32]{3,2,1,0:T(8,128)} reshape(f32[128,1024]{1,0:T(8,128)S(1)} %fusion.1) | data formatting | bytes 1048576 | tf_op jit(solution)/shard_map/reshape | solution.py:319
  12.1 3.6 %fusion = bf16[8,32,16,32]{3,2,1,0:T(8,128)(2,1)S(1)} fusion(f32[8,16,32,32]{2,1,3,0:T(8,128)} %copy.14, f32[8,16,32,32]{3,2,1,0:T(8,128)} %reshape.857), kind=kLoop, calls=%fused_computation.3 | loop fusion | flops 262144 | bytes 1310720 | tf_op jit(solution)/shard_map/convert_element_type | solution.py:322
  15.7 1.0 %convert_element_type.45 = bf16[256,512]{1,0:T(8,128)(2,1)S(1)} reshape(bf16[8,32,16,32]{3,2,1,0:T(8,128)(2,1)S(1)} %fusion) | data formatting | bytes 524288 | tf_op jit(solution)/shard_map/convert_element_type | solution.py:322
  16.8 0.3 copy.12
  17.1 0.1 broadcast_in_dim.114
  17.3 0.2 pad_maximum_fusion
  17.5 0.6 gather_fusion.1
  18.2 0.1 fusion.9
  18.3 0.6 gather_fusion
  18.9 0.1 fusion.18
  19.1 2.8 %collective-permute-start.4 = (bf16[800,128]{1,0:T(8,128)(2,1)S(1)}, bf16[800,128]{1,0:T(8,128)(2,1)S(1)}, u32[]{:S(2)}, u32[]{:S(2)}) collective-permute-start(bf16[800,128]{1,0:T(8,128)(2,1)S(1)} %get-tuple-element.29), channel_id=1, source_target_pairs={{0,3},{1,0},{2,1},{3,2},{4,7},{5,4},{6,5},{7,6},{8,11},{9,8},{10,9... | collective-permute-start | bytes 614408 | tf_op jit(solution)/shard_map/ppermute | solution.py:48
  22.0 0.9 collective-permute-start.5
  22.9 1.0 collective-permute-start.1
  23.8 3.7 %collective-permute-done.4 = bf16[800,128]{1,0:T(8,128)(2,1)S(1)} collective-permute-done((bf16[800,128]{1,0:T(8,128)(2,1)S(1)}, bf16[800,128]{1,0:T(8,128)(2,1)S(1)}, u32[]{:S(2)}, u32[]{:S(2)}) %collective-permute-start.4) | collective-permute-done | bytes 204832 | tf_op jit(solution)/shard_map/ppermute | solution.py:48
  27.5 1.9 %collective-permute-done.5 = bf16[800,128]{1,0:T(8,128)(2,1)S(1)} collective-permute-done((bf16[800,128]{1,0:T(8,128)(2,1)S(1)}, bf16[800,128]{1,0:T(8,128)(2,1)S(1)}, u32[]{:S(2)}, u32[]{:S(2)}) %collective-permute-start.5) | collective-permute-done | bytes 204832 | tf_op jit(solution)/shard_map/ppermute | solution.py:48
  29.4 0.8 collective-permute-start.6
  30.3 1.2 %collective-permute-done.1 = bf16[800,128]{1,0:T(8,128)(2,1)S(1)} collective-permute-done((bf16[800,128]{1,0:T(8,128)(2,1)S(1)}, bf16[800,128]{1,0:T(8,128)(2,1)S(1)}, u32[]{:S(2)}, u32[]{:S(2)}) %collective-permute-start.1) | collective-permute-done | bytes 204832 | tf_op jit(solution)/shard_map/ppermute | solution.py:48
  31.5 1.3 %collective-permute-start.2 = (bf16[1600,128]{1,0:T(8,128)(2,1)S(1)}, bf16[1600,128]{1,0:T(8,128)(2,1)S(1)}, u32[]{:S(2)}, u32[]{:S(2)}) collective-permute-start(bf16[1600,128]{1,0:T(8,128)(2,1)S(1)} %constant_dynamic-update-slice_fusion.3.refs_0_), channel_id=1, source_target_pairs={{0,4},{1,5},{2,6},{3,7},{4,8},{5,9},{6,10},{7,11},{8,12},{9,13},{1... | collective-permute-start | bytes 1228808 | tf_op jit(solution)/shard_map/ppermute | solution.py:53
  32.9 0.1 broadcast_select_fusion.sources
  33.0 0.6 collective-permute-start.8
  33.6 1.5 %collective-permute-start.9 = (bf16[1600,128]{1,0:T(8,128)(2,1)S(1)}, bf16[1600,128]{1,0:T(8,128)(2,1)S(1)}, u32[]{:S(2)}, u32[]{:S(2)}) collective-permute-start(bf16[1600,128]{1,0:T(8,128)(2,1)S(1)} %constant_dynamic-update-slice_fusion.3.refs_0_), channel_id=1, source_target_pairs={{0,12},{1,13},{2,14},{3,15},{4,0},{5,1},{6,2},{7,3},{8,4},{9,5},{1... | collective-permute-start | bytes 1228808 | tf_op jit(solution)/shard_map/ppermute | solution.py:53
  35.1 0.2 convolution_convert_fusion.counts
  35.3 3.4 %collective-permute-done.6.refs_3_ = bf16[1600,128]{1,0:T(8,128)(2,1)S(1)} collective-permute-done((bf16[1600,128]{1,0:T(8,128)(2,1)S(1)}, bf16[1600,128]{1,0:T(8,128)(2,1)S(1)}, u32[]{:S(2)}, u32[]{:S(2)}) %collective-permute-start.6) | collective-permute-done | bytes 409632 | tf_op jit(solution)/shard_map/ppermute | solution.py:53
  38.7 0.9 collective-permute-done.2.refs_0_
  39.6 2.5 %collective-permute-start.3 = (bf16[1600,128]{1,0:T(8,128)(2,1)S(1)}, bf16[1600,128]{1,0:T(8,128)(2,1)S(1)}, u32[]{:S(2)}, u32[]{:S(2)}) collective-permute-start(bf16[1600,128]{1,0:T(8,128)(2,1)S(1)} %collective-permute-done.2.refs_0_), channel_id=1, source_target_pairs={{0,4},{1,5},{2,6},{3,7},{4,8},{5,9},{6,10},{7,11},{8,12},{9,13},{1... | collective-permute-start | bytes 1228808 | tf_op jit(solution)/shard_map/ppermute | solution.py:53
  42.0 7.5 %near_from_0.1.refs_4_ = f32[8,800,128]{2,1,0:T(8,128)S(1)} custom-call(s32[8,32]{1,0:T(8,128)S(1)} %convolution_convert_fusion.counts, f32[32,4,128]{2,1,0:T(4,128)S(1)} %broadcast_select_fusion.sources, f32[8,8,256]{2,1,0:T(8,128)S(1)} %concatenate.25.targets, bf16[256,128]{1,0:T(8,128)(2,1)S(1)} %get-tuple-element.23.blocks, ...), custom_call_target="tpu_custom_call" | custom-call | flops 2000000000 | bytes 8000000 | tf_op jit(solution)/shard_map/near_from_0/pallas_call | solution.py:213
  49.5 1.7 %copy-done.2 = f32[8,800,128]{2,1,0:T(8,128)} copy-done((f32[8,800,128]{2,1,0:T(8,128)}, f32[8,800,128]{2,1,0:T(8,128)S(1)}, u32[]{:S(2)}) %copy-start.2) | copy-done | bytes 3276824
  51.2 16.4 %near_from_4.1.refs_2_ = f32[8,800,128]{2,1,0:T(8,128)S(1)} custom-call(s32[8,32]{1,0:T(8,128)S(1)} %convolution_convert_fusion.counts, f32[32,4,128]{2,1,0:T(4,128)S(1)} %broadcast_select_fusion.sources, f32[8,8,256]{2,1,0:T(8,128)S(1)} %concatenate.25.targets, bf16[256,256]{1,0:T(8,128)(2,1)S(1)} %slice.65.blocks, ...), custom_call_target="tpu_custom_call" | custom-call | flops 4000000000 | bytes 8000000 | tf_op jit(solution)/shard_map/near_from_4/pallas_call | solution.py:213
  67.7 1.7 %copy-done.1 = f32[8,800,128]{2,1,0:T(8,128)} copy-done((f32[8,800,128]{2,1,0:T(8,128)}, f32[8,800,128]{2,1,0:T(8,128)S(1)}, u32[]{:S(2)}) %copy-start.1) | copy-done | bytes 3276824
  69.3 11.1 %near_from_12.1 = (f32[4,800,128]{2,1,0:T(8,128)S(1)}, bf16[4,800,128]{2,1,0:T(8,128)(2,1)S(1)}) custom-call(s32[8,32]{1,0:T(8,128)S(1)} %convolution_convert_fusion.counts, f32[32,4,128]{2,1,0:T(4,128)S(1)} %broadcast_select_fusion.sources, f32[8,8,256]{2,1,0:T(8,128)S(1)} %concatenate.25.targets, bf16[256,128]{1,0:T(8,128)(2,1)S(1)} %get-tuple-element.24.blocks, ...), custom_call_target="tpu_custom_call" | custom-call | flops 2000000000 | bytes 8000000 | tf_op jit(solution)/shard_map/near_from_12/pallas_call | solution.py:213
  80.4 0.1 collective-permute-start.10
  80.5 2.3 %collective-permute-done.10 = bf16[4,800,128]{2,1,0:T(8,128)(2,1)S(1)} collective-permute-done((bf16[4,800,128]{2,1,0:T(8,128)(2,1)S(1)}, bf16[4,800,128]{2,1,0:T(8,128)(2,1)S(1)}, u32[]{:S(2)}, u32[]{:S(2)}) %collective-permute-start.10) | collective-permute-done | bytes 819232 | tf_op jit(solution)/shard_map/ppermute | solution.py:43
  82.8 0.9 fusion.6
  83.7 0.1 collective-permute-start.11
  83.8 3.0 %collective-permute-start.12 = (bf16[800,128]{1,0:T(8,128)(2,1)S(1)}, bf16[800,128]{1,0:T(8,128)(2,1)S(1)}, u32[]{:S(2)}, u32[]{:S(2)}) collective-permute-start(bf16[800,128]{1,0:T(8,128)(2,1)S(1)} %get-tuple-element.20), channel_id=1, source_target_pairs={{0,64},{1,65},{2,66},{3,67},{4,68},{5,69},{6,70},{7,71},{8,72},{9,... | collective-permute-start | bytes 614408 | tf_op jit(solution)/shard_map/ppermute | solution.py:57
  86.9 0.7 slice_bitcast_fusion.1.swapped
  87.6 5.2 %collective-permute-done.11.one = bf16[800,128]{1,0:T(8,128)(2,1)S(1)} collective-permute-done((bf16[800,128]{1,0:T(8,128)(2,1)S(1)}, bf16[800,128]{1,0:T(8,128)(2,1)S(1)}, u32[]{:S(2)}, u32[]{:S(2)}) %collective-permute-start.11) | collective-permute-done | bytes 204832 | tf_op jit(solution)/shard_map/ppermute | solution.py:57
  92.8 3.6 %collective-permute-done.12.two = bf16[800,128]{1,0:T(8,128)(2,1)S(1)} collective-permute-done((bf16[800,128]{1,0:T(8,128)(2,1)S(1)}, bf16[800,128]{1,0:T(8,128)(2,1)S(1)}, u32[]{:S(2)}, u32[]{:S(2)}) %collective-permute-start.12) | collective-permute-done | bytes 204832 | tf_op jit(solution)/shard_map/ppermute | solution.py:57
  96.4 0.6 collective-permute-done.13.three
  97.1 0.6 copy-done.6
  97.7 2.3 %sum_and_expand.1 = bf16[1,3,256,128]{3,2,1,0:T(8,128)(2,1)} custom-call(f32[800,128]{1,0:T(8,128)} %get-tuple-element.22.keep, bf16[800,128]{1,0:T(8,128)(2,1)} %slice_bitcast_fusion.1.swapped, bf16[800,128]{1,0:T(8,128)(2,1)} %copy-done.4, bf16[800,128]{1,0:T(8,128)(2,1)} %copy-done.5, bf16[800,128]{1,0:T(8,128)(2,1)} %copy-done.6, ...), custom_call_target="tpu_custom_call" | custom-call | tf_op jit(solution)/shard_map/sum_and_expand/pallas_call | solution.py:256
  (45 shorter events, 0.6 us)
Async XLA Ops:
  0.0 4.3 %copy-start = (bf16[768,1024]{1,0:T(8,128)(2,1)S(1)}, bf16[768,1024]{1,0:T(8,128)(2,1)}, u32[]{:S(2)}) copy-start(bf16[768,1024]{1,0:T(8,128)(2,1)} %param.13) | copy-start | bytes 4718596
  3.3 15.7 %collective-permute-start = (bf16[384,128]{1,0:T(8,128)(2,1)}, bf16[384,128]{1,0:T(8,128)(2,1)S(1)}, u32[]{:S(2)}, u32[]{:S(2)}) collective-permute-start(bf16[384,128]{1,0:T(8,128)(2,1)} %get-tuple-element.11), channel_id=1, source_target_pairs={{0,16},{1,17},{2,18},{3,19},{4,20},{5,21},{6,22},{7,23},{8,24},{9,... | collective-permute-start | bytes 294920 | tf_op jit(solution)/shard_map/ppermute | solution.py:43
  15.7 1.1 %copy-start.3 = (f32[128,3,256]{2,0,1:T(8,128)S(1)}, f32[128,3,256]{2,0,1:T(8,128)}, u32[]{:S(2)}) copy-start(f32[128,3,256]{2,0,1:T(8,128)} %param.8) | copy-start | bytes 1179652
  15.7 1.4 %copy-start.7 = (f32[128,256]{1,0:T(8,128)S(1)}, f32[128,256]{1,0:T(8,128)}, u32[]{:S(2)}) copy-start(f32[128,256]{1,0:T(8,128)} %param.9) | copy-start | bytes 393220
  15.7 1.5 %copy-start.9 = (s32[1920,2]{0,1:T(2,128)S(1)}, s32[1920,2]{0,1:T(2,128)}, u32[]{:S(2)}) copy-start(s32[1920,2]{0,1:T(2,128)} %param.11) | copy-start | bytes 46084
  16.8 2.3 %copy-start.10 = (bf16[32,128]{1,0:T(8,128)(2,1)S(1)}, bf16[32,128]{1,0:T(8,128)(2,1)}, u32[]{:S(2)}) copy-start(bf16[32,128]{1,0:T(8,128)(2,1)} %get-tuple-element.12) | copy-start | bytes 24580
  17.1 1.9 %copy-start.8 = (bf16[384,128]{1,0:T(8,128)(2,1)S(1)}, bf16[384,128]{1,0:T(8,128)(2,1)}, u32[]{:S(2)}) copy-start(bf16[384,128]{1,0:T(8,128)(2,1)} %get-tuple-element.10) | copy-start | bytes 294916
  19.1 8.3 %collective-permute-start.4 = (bf16[800,128]{1,0:T(8,128)(2,1)S(1)}, bf16[800,128]{1,0:T(8,128)(2,1)S(1)}, u32[]{:S(2)}, u32[]{:S(2)}) collective-permute-start(bf16[800,128]{1,0:T(8,128)(2,1)S(1)} %get-tuple-element.29), channel_id=1, source_target_pairs={{0,3},{1,0},{2,1},{3,2},{4,7},{5,4},{6,5},{7,6},{8,11},{9,8},{10,9... | collective-permute-start | bytes 614408 | tf_op jit(solution)/shard_map/ppermute | solution.py:48
  22.0 7.4 %collective-permute-start.5 = (bf16[800,128]{1,0:T(8,128)(2,1)S(1)}, bf16[800,128]{1,0:T(8,128)(2,1)S(1)}, u32[]{:S(2)}, u32[]{:S(2)}) collective-permute-start(bf16[800,128]{1,0:T(8,128)(2,1)S(1)} %get-tuple-element.29), channel_id=1, source_target_pairs={{0,2},{1,3},{2,0},{3,1},{4,6},{5,7},{6,4},{7,5},{8,10},{9,11},{10,... | collective-permute-start | bytes 614408 | tf_op jit(solution)/shard_map/ppermute | solution.py:48
  22.9 8.6 %collective-permute-start.1 = (bf16[800,128]{1,0:T(8,128)(2,1)S(1)}, bf16[800,128]{1,0:T(8,128)(2,1)S(1)}, u32[]{:S(2)}, u32[]{:S(2)}) collective-permute-start(bf16[800,128]{1,0:T(8,128)(2,1)S(1)} %get-tuple-element.29), channel_id=1, source_target_pairs={{0,1},{1,2},{2,3},{3,0},{4,5},{5,6},{6,7},{7,4},{8,9},{9,10},{10,1... | collective-permute-start | bytes 614408 | tf_op jit(solution)/shard_map/ppermute | solution.py:48
  29.4 9.2 %collective-permute-start.6 = (bf16[1600,128]{1,0:T(8,128)(2,1)S(1)}, bf16[1600,128]{1,0:T(8,128)(2,1)S(1)}, u32[]{:S(2)}, u32[]{:S(2)}) collective-permute-start(bf16[1600,128]{1,0:T(8,128)(2,1)S(1)} %constant_dynamic-update-slice_fusion.7.refs_1_), channel_id=1, source_target_pairs={{0,12},{1,13},{2,14},{3,15},{4,0},{5,1},{6,2},{7,3},{8,4},{9,5},{1... | collective-permute-start | bytes 1228808 | tf_op jit(solution)/shard_map/ppermute | solution.py:53
  31.5 8.0 %collective-permute-start.2 = (bf16[1600,128]{1,0:T(8,128)(2,1)S(1)}, bf16[1600,128]{1,0:T(8,128)(2,1)S(1)}, u32[]{:S(2)}, u32[]{:S(2)}) collective-permute-start(bf16[1600,128]{1,0:T(8,128)(2,1)S(1)} %constant_dynamic-update-slice_fusion.3.refs_0_), channel_id=1, source_target_pairs={{0,4},{1,5},{2,6},{3,7},{4,8},{5,9},{6,10},{7,11},{8,12},{9,13},{1... | collective-permute-start | bytes 1228808 | tf_op jit(solution)/shard_map/ppermute | solution.py:53
  33.0 18.2 %collective-permute-start.8 = (bf16[1600,128]{1,0:T(8,128)(2,1)S(1)}, bf16[1600,128]{1,0:T(8,128)(2,1)S(1)}, u32[]{:S(2)}, u32[]{:S(2)}) collective-permute-start(bf16[1600,128]{1,0:T(8,128)(2,1)S(1)} %constant_dynamic-update-slice_fusion.7.refs_1_), channel_id=1, source_target_pairs={{0,4},{1,5},{2,6},{3,7},{4,8},{5,9},{6,10},{7,11},{8,12},{9,13},{1... | collective-permute-start | bytes 1228808 | tf_op jit(solution)/shard_map/ppermute | solution.py:53
  33.6 17.6 %collective-permute-start.9 = (bf16[1600,128]{1,0:T(8,128)(2,1)S(1)}, bf16[1600,128]{1,0:T(8,128)(2,1)S(1)}, u32[]{:S(2)}, u32[]{:S(2)}) collective-permute-start(bf16[1600,128]{1,0:T(8,128)(2,1)S(1)} %constant_dynamic-update-slice_fusion.3.refs_0_), channel_id=1, source_target_pairs={{0,12},{1,13},{2,14},{3,15},{4,0},{5,1},{6,2},{7,3},{8,4},{9,5},{1... | collective-permute-start | bytes 1228808 | tf_op jit(solution)/shard_map/ppermute | solution.py:53
  38.7 30.6 %collective-permute-start.7 = (bf16[1600,128]{1,0:T(8,128)(2,1)S(1)}, bf16[1600,128]{1,0:T(8,128)(2,1)S(1)}, u32[]{:S(2)}, u32[]{:S(2)}) collective-permute-start(bf16[1600,128]{1,0:T(8,128)(2,1)S(1)} %collective-permute-done.6.refs_3_), channel_id=1, source_target_pairs={{0,12},{1,13},{2,14},{3,15},{4,0},{5,1},{6,2},{7,3},{8,4},{9,5},{1... | collective-permute-start | bytes 1228808 | tf_op jit(solution)/shard_map/ppermute | solution.py:53
  39.6 29.8 %collective-permute-start.3 = (bf16[1600,128]{1,0:T(8,128)(2,1)S(1)}, bf16[1600,128]{1,0:T(8,128)(2,1)S(1)}, u32[]{:S(2)}, u32[]{:S(2)}) collective-permute-start(bf16[1600,128]{1,0:T(8,128)(2,1)S(1)} %collective-permute-done.2.refs_0_), channel_id=1, source_target_pairs={{0,4},{1,5},{2,6},{3,7},{4,8},{5,9},{6,10},{7,11},{8,12},{9,13},{1... | collective-permute-start | bytes 1228808 | tf_op jit(solution)/shard_map/ppermute | solution.py:53
  49.5 1.7 %copy-start.2 = (f32[8,800,128]{2,1,0:T(8,128)}, f32[8,800,128]{2,1,0:T(8,128)S(1)}, u32[]{:S(2)}) copy-start(f32[8,800,128]{2,1,0:T(8,128)S(1)} %near_from_0.1.refs_4_) | copy-start | bytes 9830404
  67.7 1.7 %copy-start.1 = (f32[8,800,128]{2,1,0:T(8,128)}, f32[8,800,128]{2,1,0:T(8,128)S(1)}, u32[]{:S(2)}) copy-start(f32[8,800,128]{2,1,0:T(8,128)S(1)} %near_from_4.1.refs_2_) | copy-start | bytes 9830404
  80.4 2.4 %collective-permute-start.10 = (bf16[4,800,128]{2,1,0:T(8,128)(2,1)S(1)}, bf16[4,800,128]{2,1,0:T(8,128)(2,1)S(1)}, u32[]{:S(2)}, u32[]{:S(2)}) collective-permute-start(bf16[4,800,128]{2,1,0:T(8,128)(2,1)S(1)} %get-tuple-element.14), channel_id=1, source_target_pairs={{0,16},{1,17},{2,18},{3,19},{4,20},{5,21},{6,22},{7,23},{8,24},{9,... | collective-permute-start | bytes 2457608 | tf_op jit(solution)/shard_map/ppermute | solution.py:43
  83.7 9.1 %collective-permute-start.11 = (bf16[800,128]{1,0:T(8,128)(2,1)S(1)}, bf16[800,128]{1,0:T(8,128)(2,1)S(1)}, u32[]{:S(2)}, u32[]{:S(2)}) collective-permute-start(bf16[800,128]{1,0:T(8,128)(2,1)S(1)} %get-tuple-element.21), channel_id=1, source_target_pairs={{0,32},{1,33},{2,34},{3,35},{4,36},{5,37},{6,38},{7,39},{8,40},{9,... | collective-permute-start | bytes 614408 | tf_op jit(solution)/shard_map/ppermute | solution.py:57
  83.8 12.6 %collective-permute-start.12 = (bf16[800,128]{1,0:T(8,128)(2,1)S(1)}, bf16[800,128]{1,0:T(8,128)(2,1)S(1)}, u32[]{:S(2)}, u32[]{:S(2)}) collective-permute-start(bf16[800,128]{1,0:T(8,128)(2,1)S(1)} %get-tuple-element.20), channel_id=1, source_target_pairs={{0,64},{1,65},{2,66},{3,67},{4,68},{5,69},{6,70},{7,71},{8,72},{9,... | collective-permute-start | bytes 614408 | tf_op jit(solution)/shard_map/ppermute | solution.py:57
  86.9 10.2 %collective-permute-start.13 = (bf16[800,128]{1,0:T(8,128)(2,1)S(1)}, bf16[800,128]{1,0:T(8,128)(2,1)S(1)}, u32[]{:S(2)}, u32[]{:S(2)}) collective-permute-start(bf16[800,128]{1,0:T(8,128)(2,1)S(1)} %get-tuple-element.19), channel_id=1, source_target_pairs={{0,96},{1,97},{2,98},{3,99},{4,100},{5,101},{6,102},{7,103},{8,104... | collective-permute-start | bytes 614408 | tf_op jit(solution)/shard_map/ppermute | solution.py:57
  92.8 4.2 %copy-start.4 = (bf16[800,128]{1,0:T(8,128)(2,1)}, bf16[800,128]{1,0:T(8,128)(2,1)S(1)}, u32[]{:S(2)}) copy-start(bf16[800,128]{1,0:T(8,128)(2,1)S(1)} %collective-permute-done.11.one) | copy-start | bytes 614404
  96.4 0.7 copy-start.5
  97.0 0.7 copy-start.6

commit v2 on v1

v2 whole, which is shorter than its diff:
```python
import functools

import jax
import jax.numpy as jnp
from jax import lax
from jax.experimental import pallas as pl
from jax.experimental.pallas import tpu as pltpu
from jax.sharding import PartitionSpec as P


CS = 256
LOADS = 128
RANK = 32
HALF = CS // 2
DENS = 3 * HALF
UNIT = 2 * DENS + RANK
FULL = 3 * CS + RANK
AXES = ("row", "col")
SIDE = 4

eps_square = 0.0004
lame_ratio = 1.8
kelvin_coef = 1.0 / (16.0 * 3.141592653589793 * 0.7)
VMEM_LIMIT = 16 * 1024 * 1024
bf16 = jnp.bfloat16
f32 = jnp.float32


def routes(move):
    pairs = []
    for z in range(SIDE):
        for core in range(2):
            for y in range(SIDE):
                for x in range(SIDE):
                    to_z, to_core, to_y, to_x = move(z, core, y, x)
                    source = (z * 2 + core) * 16 + y * SIDE + x
                    target = ((to_z % SIDE) * 2 + to_core) * 16 + (to_y % SIDE) * SIDE + to_x % SIDE
                    pairs.append((source, target))
    return pairs


def swap_core(value):
    return lax.ppermute(value, AXES, routes(lambda z, c, y, x: (z, 1 - c, y, x)))


def along_first(value, step):
    move = lambda z, c, y, x: (z, c, y, x + step) if c == 0 else (z, c, y + step, x)
    return lax.ppermute(value, AXES, routes(move))


def along_second(value, step):
    move = lambda z, c, y, x: (z, c, y + step, x) if c == 0 else (z, c, y, x + step)
    return lax.ppermute(value, AXES, routes(move))


def along_z(value, step):
    return lax.ppermute(value, AXES, routes(lambda z, c, y, x: (z + step, c, y, x)))


def whole(count):
    return [pl.BlockSpec(memory_space=pltpu.VMEM)] * count


def dot32(a, b):
    return jnp.dot(a, b, preferred_element_type=f32)


def moments_kernel(dens_ref, bases_ref, moments_ref):
    total = jnp.zeros((RANK, LOADS), f32)
    for j in range(3):
        total += dot32(bases_ref[0, j], dens_ref[0, j])
    moments_ref[...] = total.astype(bf16)


def moments_of(densities, bases):
    return pl.pallas_call(
        moments_kernel,
        out_shape=jax.ShapeDtypeStruct((RANK, LOADS), bf16),
        in_specs=whole(2),
        out_specs=whole(1)[0],
        name="moments",
    )(densities, bases)


def unit_kernel(core_ref, own_ref, partner_ref, moments_ref, unit_ref):
    half = pl.ds(pl.multiple_of(core_ref[0] * HALF, HALF), HALF)
    for j in range(3):
        unit_ref[j * HALF : (j + 1) * HALF] = jnp.transpose(own_ref[0, j, half, :])
        unit_ref[DENS + j * HALF : DENS + (j + 1) * HALF] = jnp.transpose(
            partner_ref[0, j, half, :]
        )
    unit_ref[2 * DENS :] = moments_ref[...]


def make_unit(core, own, partner, moments):
    return pl.pallas_call(
        unit_kernel,
        out_shape=jax.ShapeDtypeStruct((UNIT, LOADS), bf16),
        in_specs=[pl.BlockSpec(memory_space=pltpu.SMEM)] + whole(3),
        out_specs=whole(1)[0],
        name="unit",
    )(jnp.reshape(core, (1,)), own, partner, moments)


def tables_kernel(
    here_ref, forward_ref, backward_ref, couplings_ref, positions_ref, areas_ref,
    blocks_ref, spread_ref, targets_ref, columns,
):
    z, core, y, x = (here_ref[k] for k in range(4))
    for t in range(8):
        cluster = (((t & 3) + z) & 3) * 32 + (((t >> 2) + core) & 1) * 16 + y * SIDE + x
        for i in range(3):
            targets_ref[t, i : i + 1, :] = positions_ref[i, pl.ds(cluster, 1), :]
        targets_ref[t, 3:4, :] = areas_ref[pl.ds(cluster, 1), :]
    half = lambda whole_row: jnp.where(core == 0, whole_row[:, :HALF], whole_row[:, HALF:])
    back = (0, 3, 1, 2)
    for s in range(32):
        first, second = back[(s >> 1) & 3], back[s >> 3]
        on_x = (x + jnp.where(core == 0, first, second)) & 3
        on_y = (y + jnp.where(core == 0, second, first)) & 3
        cluster = z * 32 + ((s + core) & 1) * 16 + on_y * SIDE + on_x
        for i in range(3):
            columns[s, i : i + 1, :] = half(positions_ref[i, pl.ds(cluster, 1), :])
        columns[s, 3:4, :] = half(areas_ref[pl.ds(cluster, 1), :])
    for s in range(32):
        upright = jnp.transpose(columns[s])
        for i in range(4):
            spread_ref[s, i] = jnp.broadcast_to(upright[:, i : i + 1], (HALF, LOADS))
    iota = lambda shape, dim: lax.broadcasted_iota(jnp.int32, shape, dim)
    cells, width = 128, RANK * RANK
    far = couplings_ref.shape[0]

    def summed(cell_ref):
        marks = iota((cells, far), 0) == cell_ref[...]
        return dot32(jnp.where(marks, 1.0, 0.0).astype(bf16), couplings_ref[...])

    at, to = iota((width, width), 0), iota((width, width), 1)
    flip = jnp.where((at // RANK == to % RANK) & (at % RANK == to // RANK), 1.0, 0.0)
    total = summed(forward_ref) + dot32(summed(backward_ref).astype(bf16), flip.astype(bf16))
    total = total.astype(bf16)
    columns = 16 * RANK
    row, lane = iota((cells, columns), 0), iota((cells, columns), 1)
    same_unit = row % 16 == lane // RANK
    spread = [
        jnp.where(row == lane % RANK + RANK * k, 1.0, 0.0).astype(bf16) for k in range(4)
    ]
    place, cell = iota((16, 2 * cells), 0), iota((16, 2 * cells), 1)
    gather = jnp.where(place == cell // 16, 1.0, 0.0).astype(bf16)
    for pair in range(RANK // 2):
        parts = []
        for r in (2 * pair, 2 * pair + 1):
            at = r // 4 * 128
            wide = dot32(total[:, at : at + 128], spread[r % 4])
            parts.append(jnp.where(same_unit, wide, 0.0).astype(bf16))
        both = jnp.concatenate(parts, axis=0)
        blocks_ref[pair * 16 : (pair + 1) * 16] = dot32(gather, both).astype(bf16)


def make_tables(here, forward, backward, couplings, positions, areas):
    return pl.pallas_call(
        tables_kernel,
        out_shape=(
            jax.ShapeDtypeStruct((8 * RANK, 16 * RANK), bf16),
            jax.ShapeDtypeStruct((32, 4, HALF, LOADS), f32),
            jax.ShapeDtypeStruct((8, 8, CS), f32),
        ),
        in_specs=[pl.BlockSpec(memory_space=pltpu.SMEM)] + whole(5),
        out_specs=tuple(whole(3)),
        scratch_shapes=[pltpu.VMEM((32, 8, HALF), f32)],
        compiler_params=pltpu.CompilerParams(vmem_limit_bytes=VMEM_LIMIT),
        name="tables",
    )(here, forward[None, :], backward[None, :], couplings, positions, areas)


def near_kernel(first_unit, buffers, is_first, is_last, counts, targets, spread, blocks, *refs):
    units = 2 * buffers
    slots = 2 * units
    held = refs[:buffers]
    refs = refs[buffers:]
    if not is_first:
        carried, refs = refs[0], refs[1:]
    if is_last:
        keep, send, acc, refs = refs[0], refs[1], refs[2], refs[3:]
    else:
        acc, refs = refs[0], refs[1:]
    flat, tile_a, tile_b, far, entry, sems = refs

    copies = []
    for k in range(buffers):
        place = flat.at[k * 2 * UNIT : (k + 1) * 2 * UNIT]
        copies.append(pltpu.make_async_copy(held[k], place, sems.at[k]))
        copies[-1].start()

    def list_target(t, filled):
        for value in [counts[t, 2 * first_unit + s] for s in range(slots)]:
            entry[filled] = value
            filled = filled + jnp.where(value >= 4096, 1, 0)
        entry[filled] = t * 64 + 2 * first_unit
        return filled + (filled & 1)

    entries = lax.fori_loop(0, 8, list_target, 0)
    for k in range(6):
        entry[entries + k] = 2 * first_unit
    if is_first:
        acc[:, : 3 * CS] = jnp.zeros((8, 3 * CS, LOADS), f32)
    else:
        acc[...] = carried[...]
    for copy in copies:
        copy.wait()

    moments = jnp.concatenate(
        [flat[u * UNIT + 2 * DENS : (u + 1) * UNIT, :] for u in range(units)], axis=0
    )
    far[...] = dot32(blocks[...], moments)
    for t in range(8):
        part = far[pl.ds(t, RANK, stride=8), :]
        if is_first:
            acc[t, 3 * CS :] = part
        else:
            acc[t, 3 * CS :] += part

    def decode(k):
        both = [entry[2 * k + h] for h in range(2)]
        return (both[0] >> 6) & 7, [v & 63 for v in both], [v >> 12 for v in both]

    def make_tile(k, tile):
        t, slot, pairs = decode(k)
        amount = [p.astype(f32) * kelvin_coef for p in pairs]
        point = targets[t]
        step = 16
        for at in range(0, CS, step):
            side = at // HALF
            rows = slice(at % HALF, at % HALF + step)
            here = [spread[slot[side], i, rows] for i in range(4)]
            for h in range(2):
                lanes = slice(h * HALF, (h + 1) * HALF)
                dx, dy, dz = (here[i] - point[i : i + 1, lanes] for i in range(3))
                inverse = lax.rsqrt(dx * dx + dy * dy + dz * dz + eps_square)
                scaled = (here[3] * (point[3:4, lanes] * amount[side])) * inverse
                cubed = scaled * (inverse * inverse)
                level = lame_ratio * scaled
                ex, ey, ez = dx * cubed, dy * cubed, dz * cubed
                values = (dx * ex + level, dy * ey + level, dz * ez + level, dx * ey, dx * ez, dy * ez)
                for b in range(6):
                    tile[b, at : at + step, lanes] = values[b].astype(bf16)

    def add_products(k, tile):
        t, slot, _ = decode(k)
        f = []
        for j in range(3):
            parts = []
            for h in range(2):
                base = ((slot[h] >> 1) - first_unit) * UNIT + (slot[h] & 1) * DENS + j * HALF
                parts.append(flat[pl.ds(pl.multiple_of(base, 16), HALF), :])
            f.append(jnp.concatenate(parts, axis=1))
        f = jnp.concatenate(f, axis=1)
        order = ((0, 3, 4), (3, 1, 5), (4, 5, 2))
        sums = [
            dot32(f, jnp.concatenate([tile[b] for b in order[i]], axis=0)) for i in range(3)
        ]
        for i in range(3):
            for h in range(2):
                at = (2 * i + h) * HALF
                acc[t, at : at + HALF] += sums[i][:, h * HALF : (h + 1) * HALF]

    tasks = entries >> 1

    @pl.when(tasks > 0)
    def _():
        make_tile(0, tile_a)

        def two_tasks(k, carry):
            make_tile(2 * k + 1, tile_b)
            add_products(2 * k, tile_a)

            @pl.when(2 * k + 1 < tasks)
            def _():
                make_tile(2 * k + 2, tile_a)
                add_products(2 * k + 1, tile_b)

            return carry

        lax.fori_loop(0, (tasks + 1) >> 1, two_tasks, 0)

    if is_last:
        keep[...] = acc[:4]
        send[...] = acc[4:].astype(bf16)


def near(first_unit, buffers, carried, is_last, counts, targets, spread, blocks):
    count = len(buffers)
    slots = 4 * count
    is_first = carried is None
    if is_last:
        shapes = (
            jax.ShapeDtypeStruct((4, FULL, LOADS), f32),
            jax.ShapeDtypeStruct((4, FULL, LOADS), bf16),
        )
        out_specs = tuple(whole(2))
    else:
        shapes = jax.ShapeDtypeStruct((8, FULL, LOADS), f32)
        out_specs = whole(1)[0]
    operands = [counts, targets, spread, blocks] + list(buffers)
    specs = [pl.BlockSpec(memory_space=pltpu.SMEM)] + whole(3)
    specs += [pl.BlockSpec(memory_space=pl.ANY)] * count
    if not is_first:
        operands.append(carried)
        specs += whole(1)
    return pl.pallas_call(
        functools.partial(near_kernel, first_unit, count, is_first, is_last),
        out_shape=shapes,
        in_specs=specs,
        out_specs=out_specs,
        scratch_shapes=([pltpu.VMEM((8, FULL, LOADS), f32)] if is_last else [])
        + [
            pltpu.VMEM((count * 2 * UNIT, LOADS), bf16),
            pltpu.VMEM((6, CS, CS), bf16),
            pltpu.VMEM((6, CS, CS), bf16),
            pltpu.VMEM((8 * RANK, LOADS), f32),
            pltpu.SMEM((8 * slots + 16,), jnp.int32),
            pltpu.SemaphoreType.DMA((count,)),
        ],
        compiler_params=pltpu.CompilerParams(vmem_limit_bytes=VMEM_LIMIT),
        cost_estimate=pl.CostEstimate(
            flops=count * 1_000_000_000, bytes_accessed=8_000_000, transcendentals=count * 500_000
        ),
        name=f"near_from_{first_unit}",
    )(*operands)


def finish_kernel(keep, swapped, one, two, three, bases, out):
    def total(rows):
        return (
            keep[0, rows] + swapped[0, rows].astype(f32) + one[rows].astype(f32)
            + two[rows].astype(f32) + three[rows].astype(f32)
        )

    coefficients = total(slice(3 * CS, FULL))
    high = coefficients.astype(bf16)
    low = (coefficients - high.astype(f32)).astype(bf16)
    both = jnp.concatenate([high, low], axis=0)
    for j in range(3):
        basis = bases[0, j]
        twice = jnp.concatenate([basis, basis], axis=0)
        expanded = lax.dot_general(
            twice, both, (((0,), (0,)), ((), ())), preferred_element_type=f32
        )
        for h in range(2):
            at = (2 * j + h) * HALF
            near_part = jnp.transpose(total(slice(at, at + HALF)))
            panels = slice(h * HALF, (h + 1) * HALF)
            out[0, j, panels] = (near_part + expanded[panels]).astype(bf16)


def finish(keep, swapped, others, bases):
    return pl.pallas_call(
        finish_kernel,
        out_shape=jax.ShapeDtypeStruct((1, 3, CS, LOADS), bf16),
        in_specs=[pl.BlockSpec((1, FULL, LOADS), lambda i: (0, 0, 0))] * 2
        + [pl.BlockSpec((FULL, LOADS), lambda i: (0, 0))] * 3
        + [pl.BlockSpec((1, 3, RANK, CS), lambda i: (0, 0, 0, 0))],
        out_specs=pl.BlockSpec((1, 3, CS, LOADS), lambda i: (0, 0, 0, 0)),
        grid=(1,),
        name="sum_and_expand",
    )(keep, swapped, *others, bases)


def local(densities, positions, areas, bases, near_pairs, far_pairs, couplings):
    row = lax.axis_index("row")
    col = lax.axis_index("col")
    z, core = row >> 1, row & 1
    y, x = col >> 2, col & 3
    first_at = jnp.where(core == 0, x, y)
    second_at = jnp.where(core == 0, y, x)

    def unit_of(cluster):
        on_y, on_x = (cluster >> 2) & 3, cluster & 3
        first = (jnp.where(core == 0, on_x, on_y) - first_at) & 3
        second = (jnp.where(core == 0, on_y, on_x) - second_at) & 3
        put = lambda r: jnp.where(r == 0, 0, jnp.where(r == 1, 2, jnp.where(r == 2, 3, 1)))
        return put(second) * SIDE + put(first)

    def other_core(cluster):
        return ((cluster >> 4) + core) & 1

    def slot_of(cluster):
        return jnp.where(cluster >> 5 == z, unit_of(cluster) * 2 + other_core(cluster), -1)

    def target_of(cluster):
        place = other_core(cluster) * 4 + (((cluster >> 5) - z) & 3)
        return jnp.where((cluster & 15) == col, place, -1)

    bases = jnp.transpose(bases, (0, 2, 1, 3))
    positions = jnp.transpose(positions, (1, 0, 2))

    partner = swap_core(densities)
    moments = moments_of(densities, bases)
    unit = make_unit(core, densities, partner, moments)
    from_below = along_first(unit, 1)
    from_above = along_first(unit, -1)
    from_across = along_first(unit, 2)
    near_pairs, far_pairs, couplings, positions, areas, unit = lax.optimization_barrier(
        (near_pairs, far_pairs, couplings, positions, areas, unit)
    )

    heads, tails = near_pairs[:, 0], near_pairs[:, 1]
    mark = lambda index, size: index[None, :] == jnp.arange(size, dtype=jnp.int32)[:, None]
    to_targets = jnp.concatenate(
        [target_of(heads), jnp.where(heads != tails, target_of(tails), -1)]
    )
    from_slots = jnp.concatenate([slot_of(tails), slot_of(heads)])
    counts = lax.dot_general(
        mark(to_targets, 8).astype(bf16),
        mark(from_slots, 32).astype(bf16),
        (((1,), (1,)), ((), ())),
        preferred_element_type=f32,
    ).astype(jnp.int32)
    counts = counts * 4096 + jnp.arange(8, dtype=jnp.int32)[:, None] * 64 + jnp.arange(32, dtype=jnp.int32)

    far_heads, far_tails = far_pairs[:, 0], far_pairs[:, 1]

    def cell(target, source):
        ours = (target_of(target) >= 0) & (slot_of(source) >= 0) & (other_core(source) == 0)
        return jnp.where(ours, target_of(target) * 16 + unit_of(source), -1)

    back_cell = jnp.where(far_heads != far_tails, cell(far_tails, far_heads), -1)
    here = jnp.stack([z, core, y, x]).astype(jnp.int32)
    blocks, spread, targets = make_tables(
        here, cell(far_heads, far_tails), back_cell, couplings, positions, areas
    )

    (counts, targets, spread, blocks, unit, from_below, from_above, from_across) = (
        lax.optimization_barrier(
            (counts, targets, spread, blocks, unit, from_below, from_above, from_across)
        )
    )
    tables = (counts, targets, spread)
    low = jnp.concatenate([unit, from_below], axis=0)
    high = jnp.concatenate([from_above, from_across], axis=0)
    low_below = along_second(low, 1)
    high_above = along_second(high, -1)
    high_below = along_second(high, 1)
    low_above = along_second(low, -1)
    low_across = along_second(low_below, 1)
    high_across = along_second(high_above, -1)

    part = lambda a, b: blocks[:, a * RANK : b * RANK]
    acc = near(0, (low, high), None, False, *tables, part(0, 4))
    acc = near(4, (low_below, high_below, low_above, high_above), acc, False, *tables, part(4, 12))
    keep, send = near(12, (low_across, high_across), acc, True, *tables, part(12, 16))

    swapped = swap_core(send)
    both = [(keep[k] + swapped[k].astype(f32)).astype(bf16) for k in range(1, 4)]
    others = [along_z(both[k - 1], k) for k in range(1, 4)]
    return finish(keep, swapped, others, bases)


def solution(mesh):
    return jax.shard_map(
        local,
        mesh=mesh,
        in_specs=(
            P(("row", "col"), None, None, None),
            P(),
            P(),
            P(("row", "col"), None, None, None),
            P(),
            P(),
            P(),
        ),
        out_specs=P(("row", "col"), None, None, None),
        check_vma=False,
    )
```

time: 101 us -> 75.4 us (0.75)
  the two profiles are of different devices: /device:TPU:24 before, /device:TPU:28 now
where the time goes in v2:
time: 75.4 us; the launch traced here: 74.8 us
  Pallas kernels  30.2 us (40%)
  starting transfers between devices  20.7 us (27%)
  waiting for transfers between devices  15 us (20%)
  local copies, waits for them, and re-layouts  6.39 us (8%)
  other arithmetic  2.09 us (3%)
    pallas_call x3, Pallas kernels, near(): pl.pallas_call(functools.partial(near_kernel, first_unit, count, is_first...  19.5 us
    ppermute x3, waiting for transfers between devices, along_z(): lax.ppermute(value, AXES, routes(lambda z, c, y, x: (z + step, c, y, x)))  8.9 us
    ppermute x6, starting transfers between devices, along_second(): return lax.ppermute(value, AXES, routes(move))  8.73 us
    ppermute x3, starting transfers between devices, along_z(): lax.ppermute(value, AXES, routes(lambda z, c, y, x: (z + step, c, y, x)))  8.17 us
    unnamed x20, local copies, waits for them, and re-layouts  6.31 us
    pallas_call x1, Pallas kernels, make_tables(): pl.pallas_call(tables_kernel, out_shape=(jax.ShapeDtypeStruct((8 * RANK,...  4.9 us
    ppermute x6, waiting for transfers between devices, along_second(): return lax.ppermute(value, AXES, routes(move))  3.8 us
    ppermute x3, starting transfers between devices, along_first(): return lax.ppermute(value, AXES, routes(move))  3.74 us
  transfers between devices with their start and end apart: 14, of which 4 were waited for; matrix products, arithmetic and copies ran while one was open for 3% of the time, Pallas kernels for 28%

profile of v2, /device:TPU:28, one launch (start us, length us, event | category | flops | bytes accessed | tf_op | source)
XLA Modules:
  0.0 74.8 jit_solution(183570838114928350)
XLA Ops:
  0.0 0.0 collective-permute-start
  0.0 1.7 %moments.1.moments_ref = bf16[32,128]{1,0:T(8,128)(2,1)} custom-call(bf16[1,3,256,128]{3,2,1,0:T(8,128)(2,1)} %own_ref.1, bf16[1,3,32,256]{3,2,1,0:T(8,128)(2,1)} %bitcast.88), custom_call_target="tpu_custom_call" | custom-call | tf_op jit(solution)/shard_map/moments/pallas_call | solution.py:76
  1.7 0.1 pad_add_fusion.2.here_ref
  1.8 0.0 collective-permute-done.partner_ref
  1.8 0.7 copy-done.8
  2.5 1.8 %unit.1 = bf16[800,128]{1,0:T(8,128)(2,1)} custom-call(s32[1]{0:T(128)} %bitcast.1.core_ref, bf16[1,3,256,128]{3,2,1,0:T(8,128)(2,1)} %own_ref.1, bf16[1,3,256,128]{3,2,1,0:T(8,128)(2,1)} %copy-done.8, bf16[32,128]{1,0:T(8,128)(2,1)} %moments.1.moments_ref), custom_call_target="tpu_custom_call" | custom-call | tf_op jit(solution)/shard_map/unit/pallas_call | solution.py:96
  4.3 1.2 %collective-permute-start.1 = (bf16[800,128]{1,0:T(8,128)(2,1)}, bf16[800,128]{1,0:T(8,128)(2,1)S(1)}, u32[]{:S(2)}, u32[]{:S(2)}) collective-permute-start(bf16[800,128]{1,0:T(8,128)(2,1)} %unit.1), channel_id=1, source_target_pairs={{0,1},{1,2},{2,3},{3,0},{4,5},{5,6},{6,7},{7,4},{8,9},{9,10},{10,1... | collective-permute-start | bytes 614408 | tf_op jit(solution)/shard_map/ppermute | solution.py:48
  5.5 0.8 %collective-permute-start.2 = (bf16[800,128]{1,0:T(8,128)(2,1)}, bf16[800,128]{1,0:T(8,128)(2,1)S(1)}, u32[]{:S(2)}, u32[]{:S(2)}) collective-permute-start(bf16[800,128]{1,0:T(8,128)(2,1)} %unit.1), channel_id=1, source_target_pairs={{0,3},{1,0},{2,1},{3,2},{4,7},{5,4},{6,5},{7,6},{8,11},{9,8},{10,9... | collective-permute-start | bytes 614408 | tf_op jit(solution)/shard_map/ppermute | solution.py:48
  6.3 1.7 %collective-permute-start.3 = (bf16[800,128]{1,0:T(8,128)(2,1)}, bf16[800,128]{1,0:T(8,128)(2,1)S(1)}, u32[]{:S(2)}, u32[]{:S(2)}) collective-permute-start(bf16[800,128]{1,0:T(8,128)(2,1)} %unit.1), channel_id=1, source_target_pairs={{0,2},{1,3},{2,0},{3,1},{4,6},{5,7},{6,4},{7,5},{8,10},{9,11},{10,... | collective-permute-start | bytes 614408 | tf_op jit(solution)/shard_map/ppermute | solution.py:48
  8.0 0.8 %bitcast_select_fusion.2 = (s32[1,768]{1,0:T(1,128)S(1)}, s32[1,768]{1,0:T(1,128)S(1)}) fusion(pred[]{:T(512)S(6)} %eq.332, s32[]{:T(128)S(6)} %select_n.362, s32[]{:T(128)S(6)} %select_n.357, s32[]{:T(128)} %shift_right_arithmetic.130, s32[768,2]{0,1:T(2,128)} %param.12, s32[]{:T(128)} %and.294, s32[]{:T(128)S(6)} %axis_index.25), kind=kLoop, calls=%fused_computation.39 | loop fusion | flops 72192 | bytes 12309 | tf_op jit(solution)/shard_map/jit(_where)/select_n | solution.py:426
  8.9 1.0 %fusion.16 = (s32[1920]{0:T(1024)S(1)}, s32[1920]{0:T(1024)S(1)}, s32[1920]{0:T(1024)S(1)}, s32[1920]{0:T(1024)S(1)}) fusion(s32[]{:T(128)} %shift_right_arithmetic.130, s32[]{:T(128)} %and.294, s32[]{:T(128)S(6)} %axis_index.25, s32[1920,2]{0,1:T(2,128)} %param.11, s32[]{:T(128)S(6)} %select_n.362, s32[]{:T(128)S(6)} %select_n.357, pred[]{:T(512)S(6)} %eq.332), kind=kLoop, calls=%fused_computation.68 | loop fusion | flops 149760 | bytes 46101 | tf_op jit(solution)/shard_map/jit(_where)/select_n | solution.py:391
  9.9 0.0 copy-start.1
  9.9 1.4 %copy-done.1 = bf16[768,1024]{1,0:T(8,128)(2,1)S(1)} copy-done((bf16[768,1024]{1,0:T(8,128)(2,1)S(1)}, bf16[768,1024]{1,0:T(8,128)(2,1)}, u32[]{:S(2)}) %copy-start.1) | copy-done | bytes 1572888
  11.3 1.0 %copy-done.2 = f32[128,3,256]{2,0,1:T(8,128)S(1)} copy-done((f32[128,3,256]{2,0,1:T(8,128)S(1)}, f32[128,3,256]{2,0,1:T(8,128)}, u32[]{:S(2)}) %copy-start.2) | copy-done | bytes 393240
  12.3 0.9 %copy-done.3 = f32[128,256]{1,0:T(8,128)S(1)} copy-done((f32[128,256]{1,0:T(8,128)S(1)}, f32[128,256]{1,0:T(8,128)}, u32[]{:S(2)}) %copy-start.3) | copy-done | bytes 131096
  13.2 4.9 %tables.1 = (bf16[256,512]{1,0:T(8,128)(2,1)S(1)}, f32[32,4,128,128]{3,2,1,0:T(8,128)S(1)}, f32[8,8,256]{2,1,0:T(8,128)S(1)}) custom-call(s32[4]{0:T(128)S(1)} %pad_add_fusion.2.here_ref, s32[1,768]{1,0:T(1,128)S(1)} %get-tuple-element.53.forward_ref, s32[1,768]{1,0:T(1,128)S(1)} %get-tuple-element.52.backward_ref, bf16[768,1024]{1,0:T(8,128)(2,1)S(1)} %copy-done.1, ...), custom_call_target="tpu_custom_call" | custom-call | tf_op jit(solution)/shard_map/tables/pallas_call | solution.py:160
  18.1 0.2 fusion.2.counts
  18.3 0.0 collective-permute-done.1
  18.3 0.0 collective-permute-done.2
  18.4 0.0 collective-permute-done.3
  18.4 0.9 %constant_dynamic-update-slice_fusion.1 = bf16[1600,128]{1,0:T(8,128)(2,1)S(1)} fusion(bf16[800,128]{1,0:T(8,128)(2,1)} %unit.1), kind=kLoop, calls=%fused_computation.57 | loop fusion | bytes 409600
  19.4 0.8 %collective-permute-start.6 = (bf16[1600,128]{1,0:T(8,128)(2,1)S(1)}, bf16[1600,128]{1,0:T(8,128)(2,1)S(1)}, u32[]{:S(2)}, u32[]{:S(2)}) collective-permute-start(bf16[1600,128]{1,0:T(8,128)(2,1)S(1)} %constant_dynamic-update-slice_fusion.2.refs_1_), channel_id=1, source_target_pairs={{0,12},{1,13},{2,14},{3,15},{4,0},{5,1},{6,2},{7,3},{8,4},{9,5},{1... | collective-permute-start | bytes 1228808 | tf_op jit(solution)/shard_map/ppermute | solution.py:53
  20.2 2.6 %collective-permute-start.4 = (bf16[1600,128]{1,0:T(8,128)(2,1)S(1)}, bf16[1600,128]{1,0:T(8,128)(2,1)S(1)}, u32[]{:S(2)}, u32[]{:S(2)}) collective-permute-start(bf16[1600,128]{1,0:T(8,128)(2,1)S(1)} %constant_dynamic-update-slice_fusion.refs_0_), channel_id=1, source_target_pairs={{0,4},{1,5},{2,6},{3,7},{4,8},{5,9},{6,10},{7,11},{8,12},{9,13},{1... | collective-permute-start | bytes 1228808 | tf_op jit(solution)/shard_map/ppermute | solution.py:53
  22.8 0.1 collective-permute-start.8
  22.9 1.9 %collective-permute-start.9 = (bf16[1600,128]{1,0:T(8,128)(2,1)S(1)}, bf16[1600,128]{1,0:T(8,128)(2,1)S(1)}, u32[]{:S(2)}, u32[]{:S(2)}) collective-permute-start(bf16[1600,128]{1,0:T(8,128)(2,1)S(1)} %constant_dynamic-update-slice_fusion.refs_0_), channel_id=1, source_target_pairs={{0,12},{1,13},{2,14},{3,15},{4,0},{5,1},{6,2},{7,3},{8,4},{9,5},{1... | collective-permute-start | bytes 1228808 | tf_op jit(solution)/shard_map/ppermute | solution.py:53
  24.8 3.8 %collective-permute-done.6.refs_3_ = bf16[1600,128]{1,0:T(8,128)(2,1)S(1)} collective-permute-done((bf16[1600,128]{1,0:T(8,128)(2,1)S(1)}, bf16[1600,128]{1,0:T(8,128)(2,1)S(1)}, u32[]{:S(2)}, u32[]{:S(2)}) %collective-permute-start.6) | collective-permute-done | bytes 409632 | tf_op jit(solution)/shard_map/ppermute | solution.py:53
  28.6 0.0 collective-permute-start.7
  28.6 0.0 collective-permute-done.4.refs_0_
  28.6 3.3 %collective-permute-start.5 = (bf16[1600,128]{1,0:T(8,128)(2,1)S(1)}, bf16[1600,128]{1,0:T(8,128)(2,1)S(1)}, u32[]{:S(2)}, u32[]{:S(2)}) collective-permute-start(bf16[1600,128]{1,0:T(8,128)(2,1)S(1)} %collective-permute-done.4.refs_0_), channel_id=1, source_target_pairs={{0,4},{1,5},{2,6},{3,7},{4,8},{5,9},{6,10},{7,11},{8,12},{9,13},{1... | collective-permute-start | bytes 1228808 | tf_op jit(solution)/shard_map/ppermute | solution.py:53
  31.9 5.4 %near_from_0.1.refs_4_ = f32[8,800,128]{2,1,0:T(8,128)S(1)} custom-call(s32[8,32]{1,0:T(8,128)S(1)} %fusion.2.counts, f32[8,8,256]{2,1,0:T(8,128)S(1)} %get-tuple-element.34.targets, f32[32,4,128,128]{3,2,1,0:T(8,128)S(1)} %get-tuple-element.35.spread, bf16[256,128]{1,0:T(8,128)(2,1)S(1)} %get-tuple-element.50.blocks, ...), custom_call_target="tpu_custom_call" | custom-call | flops 2000000000 | bytes 8000000 | tf_op jit(solution)/shard_map/near_from_0/pallas_call | solution.py:309
  37.4 0.0 collective-permute-done.8.refs_1_
  37.4 0.0 collective-permute-done.9.refs_2_
  37.4 9.2 %near_from_4.1.refs_2_ = f32[8,800,128]{2,1,0:T(8,128)S(1)} custom-call(s32[8,32]{1,0:T(8,128)S(1)} %fusion.2.counts, f32[8,8,256]{2,1,0:T(8,128)S(1)} %get-tuple-element.34.targets, f32[32,4,128,128]{3,2,1,0:T(8,128)S(1)} %get-tuple-element.35.spread, bf16[256,256]{1,0:T(8,128)(2,1)S(1)} %slice.44.blocks, ...), custom_call_target="tpu_custom_call" | custom-call | flops 4000000000 | bytes 8000000 | tf_op jit(solution)/shard_map/near_from_4/pallas_call | solution.py:309
  46.7 0.0 collective-permute-done.7.refs_1_
  46.7 0.0 collective-permute-done.5.refs_0_
  46.7 4.9 %near_from_12.1 = (f32[4,800,128]{2,1,0:T(8,128)S(1)}, bf16[4,800,128]{2,1,0:T(8,128)(2,1)S(1)}) custom-call(s32[8,32]{1,0:T(8,128)S(1)} %fusion.2.counts, f32[8,8,256]{2,1,0:T(8,128)S(1)} %get-tuple-element.34.targets, f32[32,4,128,128]{3,2,1,0:T(8,128)S(1)} %get-tuple-element.35.spread, bf16[256,128]{1,0:T(8,128)(2,1)S(1)} %get-tuple-element.51.blocks, ...), custom_call_target="tpu_custom_call" | custom-call | flops 2000000000 | bytes 8000000 | tf_op jit(solution)/shard_map/near_from_12/pallas_call | solution.py:309
  51.6 0.1 collective-permute-start.10
  51.7 2.3 %collective-permute-done.10.swapped = bf16[4,800,128]{2,1,0:T(8,128)(2,1)S(1)} collective-permute-done((bf16[4,800,128]{2,1,0:T(8,128)(2,1)S(1)}, bf16[4,800,128]{2,1,0:T(8,128)(2,1)S(1)}, u32[]{:S(2)}, u32[]{:S(2)}) %collective-permute-start.10) | collective-permute-done | bytes 819232 | tf_op jit(solution)/shard_map/ppermute | solution.py:43
  54.0 0.1 fusion.6
  54.1 3.2 %collective-permute-start.11 = (bf16[800,128]{1,0:T(8,128)(2,1)S(1)}, bf16[800,128]{1,0:T(8,128)(2,1)S(1)}, u32[]{:S(2)}, u32[]{:S(2)}) collective-permute-start(bf16[800,128]{1,0:T(8,128)(2,1)S(1)} %get-tuple-element.49), channel_id=1, source_target_pairs={{0,32},{1,33},{2,34},{3,35},{4,36},{5,37},{6,38},{7,39},{8,40},{9,... | collective-permute-start | bytes 614408 | tf_op jit(solution)/shard_map/ppermute | solution.py:57
  57.3 4.4 %collective-permute-start.12 = (bf16[800,128]{1,0:T(8,128)(2,1)S(1)}, bf16[800,128]{1,0:T(8,128)(2,1)S(1)}, u32[]{:S(2)}, u32[]{:S(2)}) collective-permute-start(bf16[800,128]{1,0:T(8,128)(2,1)S(1)} %get-tuple-element.48), channel_id=1, source_target_pairs={{0,64},{1,65},{2,66},{3,67},{4,68},{5,69},{6,70},{7,71},{8,72},{9,... | collective-permute-start | bytes 614408 | tf_op jit(solution)/shard_map/ppermute | solution.py:57
  61.7 0.6 collective-permute-start.13
  62.3 3.3 %collective-permute-done.11.one = bf16[800,128]{1,0:T(8,128)(2,1)S(1)} collective-permute-done((bf16[800,128]{1,0:T(8,128)(2,1)S(1)}, bf16[800,128]{1,0:T(8,128)(2,1)S(1)}, u32[]{:S(2)}, u32[]{:S(2)}) %collective-permute-start.11) | collective-permute-done | bytes 204832 | tf_op jit(solution)/shard_map/ppermute | solution.py:57
  65.6 5.6 %collective-permute-done.12.two = bf16[800,128]{1,0:T(8,128)(2,1)S(1)} collective-permute-done((bf16[800,128]{1,0:T(8,128)(2,1)S(1)}, bf16[800,128]{1,0:T(8,128)(2,1)S(1)}, u32[]{:S(2)}, u32[]{:S(2)}) %collective-permute-start.12) | collective-permute-done | bytes 204832 | tf_op jit(solution)/shard_map/ppermute | solution.py:57
  71.2 0.0 collective-permute-done.13.three
  71.2 0.7 copy-done.6
  71.9 0.7 copy-done.7
  72.6 2.2 %sum_and_expand.1 = bf16[1,3,256,128]{3,2,1,0:T(8,128)(2,1)} custom-call(f32[4,800,128]{2,1,0:T(8,128)} %copy-done, bf16[4,800,128]{2,1,0:T(8,128)(2,1)} %copy-done.4, bf16[800,128]{1,0:T(8,128)(2,1)} %copy-done.5, bf16[800,128]{1,0:T(8,128)(2,1)} %copy-done.6, bf16[800,128]{1,0:T(8,128)(2,1)} %copy-done.7, bf16[1,3,32,256]{3,2,1,0:T(8,128)(2,1)} %bitcast.89), custom_call_target="tpu_custom_call" | custom-call | tf_op jit(solution)/shard_map/sum_and_expand/pallas_call | solution.py:356
  (18 shorter events, 0.1 us)
Async XLA Ops:
  0.0 1.8 %collective-permute-start = (bf16[1,3,256,128]{3,2,1,0:T(8,128)(2,1)}, bf16[1,3,256,128]{3,2,1,0:T(8,128)(2,1)S(1)}, u32[]{:S(2)}, u32[]{:S(2)}) collective-permute-start(bf16[1,3,256,128]{3,2,1,0:T(8,128)(2,1)} %own_ref.1), channel_id=1, source_target_pairs={{0,16},{1,17},{2,18},{3,19},{4,20},{5,21},{6,22},{7,23},{8,24},{9,... | collective-permute-start | bytes 589832 | tf_op jit(solution)/shard_map/ppermute | solution.py:43
  1.8 0.7 copy-start.8
  4.3 14.1 %collective-permute-start.1 = (bf16[800,128]{1,0:T(8,128)(2,1)}, bf16[800,128]{1,0:T(8,128)(2,1)S(1)}, u32[]{:S(2)}, u32[]{:S(2)}) collective-permute-start(bf16[800,128]{1,0:T(8,128)(2,1)} %unit.1), channel_id=1, source_target_pairs={{0,1},{1,2},{2,3},{3,0},{4,5},{5,6},{6,7},{7,4},{8,9},{9,10},{10,1... | collective-permute-start | bytes 614408 | tf_op jit(solution)/shard_map/ppermute | solution.py:48
  5.5 12.9 %collective-permute-start.2 = (bf16[800,128]{1,0:T(8,128)(2,1)}, bf16[800,128]{1,0:T(8,128)(2,1)S(1)}, u32[]{:S(2)}, u32[]{:S(2)}) collective-permute-start(bf16[800,128]{1,0:T(8,128)(2,1)} %unit.1), channel_id=1, source_target_pairs={{0,3},{1,0},{2,1},{3,2},{4,7},{5,4},{6,5},{7,6},{8,11},{9,8},{10,9... | collective-permute-start | bytes 614408 | tf_op jit(solution)/shard_map/ppermute | solution.py:48
  6.3 12.1 %collective-permute-start.3 = (bf16[800,128]{1,0:T(8,128)(2,1)}, bf16[800,128]{1,0:T(8,128)(2,1)S(1)}, u32[]{:S(2)}, u32[]{:S(2)}) collective-permute-start(bf16[800,128]{1,0:T(8,128)(2,1)} %unit.1), channel_id=1, source_target_pairs={{0,2},{1,3},{2,0},{3,1},{4,6},{5,7},{6,4},{7,5},{8,10},{9,11},{10,... | collective-permute-start | bytes 614408 | tf_op jit(solution)/shard_map/ppermute | solution.py:48
  9.9 1.4 %copy-start.1 = (bf16[768,1024]{1,0:T(8,128)(2,1)S(1)}, bf16[768,1024]{1,0:T(8,128)(2,1)}, u32[]{:S(2)}) copy-start(bf16[768,1024]{1,0:T(8,128)(2,1)} %couplings_ref) | copy-start | bytes 4718596
  11.3 1.0 %copy-start.2 = (f32[128,3,256]{2,0,1:T(8,128)S(1)}, f32[128,3,256]{2,0,1:T(8,128)}, u32[]{:S(2)}) copy-start(f32[128,3,256]{2,0,1:T(8,128)} %param.8) | copy-start | bytes 1179652
  12.3 0.9 %copy-start.3 = (f32[128,256]{1,0:T(8,128)S(1)}, f32[128,256]{1,0:T(8,128)}, u32[]{:S(2)}) copy-start(f32[128,256]{1,0:T(8,128)} %areas_ref) | copy-start | bytes 393220
  19.4 9.2 %collective-permute-start.6 = (bf16[1600,128]{1,0:T(8,128)(2,1)S(1)}, bf16[1600,128]{1,0:T(8,128)(2,1)S(1)}, u32[]{:S(2)}, u32[]{:S(2)}) collective-permute-start(bf16[1600,128]{1,0:T(8,128)(2,1)S(1)} %constant_dynamic-update-slice_fusion.2.refs_1_), channel_id=1, source_target_pairs={{0,12},{1,13},{2,14},{3,15},{4,0},{5,1},{6,2},{7,3},{8,4},{9,5},{1... | collective-permute-start | bytes 1228808 | tf_op jit(solution)/shard_map/ppermute | solution.py:53
  20.2 8.4 %collective-permute-start.4 = (bf16[1600,128]{1,0:T(8,128)(2,1)S(1)}, bf16[1600,128]{1,0:T(8,128)(2,1)S(1)}, u32[]{:S(2)}, u32[]{:S(2)}) collective-permute-start(bf16[1600,128]{1,0:T(8,128)(2,1)S(1)} %constant_dynamic-update-slice_fusion.refs_0_), channel_id=1, source_target_pairs={{0,4},{1,5},{2,6},{3,7},{4,8},{5,9},{6,10},{7,11},{8,12},{9,13},{1... | collective-permute-start | bytes 1228808 | tf_op jit(solution)/shard_map/ppermute | solution.py:53
  22.8 14.6 %collective-permute-start.8 = (bf16[1600,128]{1,0:T(8,128)(2,1)S(1)}, bf16[1600,128]{1,0:T(8,128)(2,1)S(1)}, u32[]{:S(2)}, u32[]{:S(2)}) collective-permute-start(bf16[1600,128]{1,0:T(8,128)(2,1)S(1)} %constant_dynamic-update-slice_fusion.2.refs_1_), channel_id=1, source_target_pairs={{0,4},{1,5},{2,6},{3,7},{4,8},{5,9},{6,10},{7,11},{8,12},{9,13},{1... | collective-permute-start | bytes 1228808 | tf_op jit(solution)/shard_map/ppermute | solution.py:53
  22.9 14.6 %collective-permute-start.9 = (bf16[1600,128]{1,0:T(8,128)(2,1)S(1)}, bf16[1600,128]{1,0:T(8,128)(2,1)S(1)}, u32[]{:S(2)}, u32[]{:S(2)}) collective-permute-start(bf16[1600,128]{1,0:T(8,128)(2,1)S(1)} %constant_dynamic-update-slice_fusion.refs_0_), channel_id=1, source_target_pairs={{0,12},{1,13},{2,14},{3,15},{4,0},{5,1},{6,2},{7,3},{8,4},{9,5},{1... | collective-permute-start | bytes 1228808 | tf_op jit(solution)/shard_map/ppermute | solution.py:53
  28.6 18.1 %collective-permute-start.7 = (bf16[1600,128]{1,0:T(8,128)(2,1)S(1)}, bf16[1600,128]{1,0:T(8,128)(2,1)S(1)}, u32[]{:S(2)}, u32[]{:S(2)}) collective-permute-start(bf16[1600,128]{1,0:T(8,128)(2,1)S(1)} %collective-permute-done.6.refs_3_), channel_id=1, source_target_pairs={{0,12},{1,13},{2,14},{3,15},{4,0},{5,1},{6,2},{7,3},{8,4},{9,5},{1... | collective-permute-start | bytes 1228808 | tf_op jit(solution)/shard_map/ppermute | solution.py:53
  28.6 18.1 %collective-permute-start.5 = (bf16[1600,128]{1,0:T(8,128)(2,1)S(1)}, bf16[1600,128]{1,0:T(8,128)(2,1)S(1)}, u32[]{:S(2)}, u32[]{:S(2)}) collective-permute-start(bf16[1600,128]{1,0:T(8,128)(2,1)S(1)} %collective-permute-done.4.refs_0_), channel_id=1, source_target_pairs={{0,4},{1,5},{2,6},{3,7},{4,8},{5,9},{6,10},{7,11},{8,12},{9,13},{1... | collective-permute-start | bytes 1228808 | tf_op jit(solution)/shard_map/ppermute | solution.py:53
  51.6 19.6 %copy-start = (f32[4,800,128]{2,1,0:T(8,128)}, f32[4,800,128]{2,1,0:T(8,128)S(1)}, u32[]{:S(2)}) copy-start(f32[4,800,128]{2,1,0:T(8,128)S(1)} %get-tuple-element.41.keep) | copy-start | bytes 4915204
  51.6 2.4 %collective-permute-start.10 = (bf16[4,800,128]{2,1,0:T(8,128)(2,1)S(1)}, bf16[4,800,128]{2,1,0:T(8,128)(2,1)S(1)}, u32[]{:S(2)}, u32[]{:S(2)}) collective-permute-start(bf16[4,800,128]{2,1,0:T(8,128)(2,1)S(1)} %get-tuple-element.42), channel_id=1, source_target_pairs={{0,16},{1,17},{2,18},{3,19},{4,20},{5,21},{6,22},{7,23},{8,24},{9,... | collective-permute-start | bytes 2457608 | tf_op jit(solution)/shard_map/ppermute | solution.py:43
  54.0 17.2 %copy-start.4 = (bf16[4,800,128]{2,1,0:T(8,128)(2,1)}, bf16[4,800,128]{2,1,0:T(8,128)(2,1)S(1)}, u32[]{:S(2)}) copy-start(bf16[4,800,128]{2,1,0:T(8,128)(2,1)S(1)} %collective-permute-done.10.swapped) | copy-start | bytes 2457604
  54.1 11.5 %collective-permute-start.11 = (bf16[800,128]{1,0:T(8,128)(2,1)S(1)}, bf16[800,128]{1,0:T(8,128)(2,1)S(1)}, u32[]{:S(2)}, u32[]{:S(2)}) collective-permute-start(bf16[800,128]{1,0:T(8,128)(2,1)S(1)} %get-tuple-element.49), channel_id=1, source_target_pairs={{0,32},{1,33},{2,34},{3,35},{4,36},{5,37},{6,38},{7,39},{8,40},{9,... | collective-permute-start | bytes 614408 | tf_op jit(solution)/shard_map/ppermute | solution.py:57
  57.3 13.9 %collective-permute-start.12 = (bf16[800,128]{1,0:T(8,128)(2,1)S(1)}, bf16[800,128]{1,0:T(8,128)(2,1)S(1)}, u32[]{:S(2)}, u32[]{:S(2)}) collective-permute-start(bf16[800,128]{1,0:T(8,128)(2,1)S(1)} %get-tuple-element.48), channel_id=1, source_target_pairs={{0,64},{1,65},{2,66},{3,67},{4,68},{5,69},{6,70},{7,71},{8,72},{9,... | collective-permute-start | bytes 614408 | tf_op jit(solution)/shard_map/ppermute | solution.py:57
  61.7 9.5 %collective-permute-start.13 = (bf16[800,128]{1,0:T(8,128)(2,1)S(1)}, bf16[800,128]{1,0:T(8,128)(2,1)S(1)}, u32[]{:S(2)}, u32[]{:S(2)}) collective-permute-start(bf16[800,128]{1,0:T(8,128)(2,1)S(1)} %get-tuple-element.47), channel_id=1, source_target_pairs={{0,96},{1,97},{2,98},{3,99},{4,100},{5,101},{6,102},{7,103},{8,104... | collective-permute-start | bytes 614408 | tf_op jit(solution)/shard_map/ppermute | solution.py:57
  65.6 5.6 %copy-start.5 = (bf16[800,128]{1,0:T(8,128)(2,1)}, bf16[800,128]{1,0:T(8,128)(2,1)S(1)}, u32[]{:S(2)}) copy-start(bf16[800,128]{1,0:T(8,128)(2,1)S(1)} %collective-permute-done.11.one) | copy-start | bytes 614404
  71.2 0.7 copy-start.6
  71.9 0.7 copy-start.7

commit v3 on v2

--- a/solution.py
+++ b/solution.py
@@ -65,27 +65,63 @@
     return jnp.dot(a, b, preferred_element_type=f32)
 
 
-def moments_kernel(dens_ref, bases_ref, moments_ref):
+def iota(shape, dim):
+    return lax.broadcasted_iota(jnp.int32, shape, dim)
+
+
+def fetch(source, target, sem):
+    copy = pltpu.make_async_copy(source, target, sem)
+    copy.start()
+    return copy
+
+
+def moments_kernel(core_ref, dens_ref, bases_ref, own_ref, moments_ref, flip_ref, dens, bases, sems):
+    copies = [fetch(dens_ref, dens, sems.at[0]), fetch(bases_ref, bases, sems.at[1])]
+    width = RANK * RANK
+    step = 128
+    for at in range(0, width, step):
+        source, target = iota((step, width), 0) + at, iota((step, width), 1)
+        turned = ((target & (RANK - 1)) << 5) + (target >> 5)
+        flip_ref[at : at + step] = jnp.where(source == turned, 1.0, 0.0).astype(bf16)
+    half = pl.ds(pl.multiple_of(core_ref[0] * HALF, HALF), HALF)
     total = jnp.zeros((RANK, LOADS), f32)
+    for copy in copies:
+        copy.wait()
     for j in range(3):
-        total += dot32(bases_ref[0, j], dens_ref[0, j])
+        total += dot32(bases[0, j], dens[0, j])
+        own_ref[j * HALF : (j + 1) * HALF] = jnp.transpose(dens[0, j, half, :])
     moments_ref[...] = total.astype(bf16)
 
 
-def moments_of(densities, bases):
+def in_hbm(array):
+    return pltpu.with_memory_space_constraint(array, pltpu.HBM)
+
+
+def moments_of(core, densities, bases):
+    width = RANK * RANK
     return pl.pallas_call(
         moments_kernel,
-        out_shape=jax.ShapeDtypeStruct((RANK, LOADS), bf16),
-        in_specs=whole(2),
-        out_specs=whole(1)[0],
+        out_shape=(
+            jax.ShapeDtypeStruct((DENS, LOADS), bf16),
+            jax.ShapeDtypeStruct((RANK, LOADS), bf16),
+            jax.ShapeDtypeStruct((width, width), bf16),
+        ),
+        in_specs=[pl.BlockSpec(memory_space=pltpu.SMEM)] + [pl.BlockSpec(memory_space=pltpu.HBM)] * 2,
+        out_specs=tuple(whole(3)),
+        scratch_shapes=[
+            pltpu.VMEM(densities.shape, bf16),
+            pltpu.VMEM(bases.shape, bf16),
+            pltpu.SemaphoreType.DMA((2,)),
+        ],
+        compiler_params=pltpu.CompilerParams(vmem_limit_bytes=VMEM_LIMIT),
         name="moments",
-    )(densities, bases)
+    )(jnp.reshape(core, (1,)), in_hbm(densities), in_hbm(bases))
 
 
 def unit_kernel(core_ref, own_ref, partner_ref, moments_ref, unit_ref):
     half = pl.ds(pl.multiple_of(core_ref[0] * HALF, HALF), HALF)
+    unit_ref[:DENS] = own_ref[...]
     for j in range(3):
-        unit_ref[j * HALF : (j + 1) * HALF] = jnp.transpose(own_ref[0, j, half, :])
         unit_ref[DENS + j * HALF : DENS + (j + 1) * HALF] = jnp.transpose(
             partner_ref[0, j, half, :]
         )
@@ -98,54 +134,79 @@
         out_shape=jax.ShapeDtypeStruct((UNIT, LOADS), bf16),
         in_specs=[pl.BlockSpec(memory_space=pltpu.SMEM)] + whole(3),
         out_specs=whole(1)[0],
+        compiler_params=pltpu.CompilerParams(vmem_limit_bytes=VMEM_LIMIT),
         name="unit",
     )(jnp.reshape(core, (1,)), own, partner, moments)
 
 
-def tables_kernel(
-    here_ref, forward_ref, backward_ref, couplings_ref, positions_ref, areas_ref,
-    blocks_ref, spread_ref, targets_ref, columns,
+def points_kernel(
+    here_ref, positions_ref, areas_ref, couplings_ref,
+    spread_ref, targets_ref, held_couplings, columns, positions, areas, sems,
 ):
+    first = [fetch(positions_ref, positions, sems.at[0]), fetch(areas_ref, areas, sems.at[1])]
+    last = fetch(couplings_ref, held_couplings, sems.at[2])
     z, core, y, x = (here_ref[k] for k in range(4))
+    half = lambda whole_row: jnp.where(core == 0, whole_row[:, :HALF], whole_row[:, HALF:])
+    back = (0, 3, 1, 2)
+    for copy in first:
+        copy.wait()
     for t in range(8):
         cluster = (((t & 3) + z) & 3) * 32 + (((t >> 2) + core) & 1) * 16 + y * SIDE + x
         for i in range(3):
-            targets_ref[t, i : i + 1, :] = positions_ref[i, pl.ds(cluster, 1), :]
-        targets_ref[t, 3:4, :] = areas_ref[pl.ds(cluster, 1), :]
-    half = lambda whole_row: jnp.where(core == 0, whole_row[:, :HALF], whole_row[:, HALF:])
-    back = (0, 3, 1, 2)
+            targets_ref[t, i : i + 1, :] = positions[i, pl.ds(cluster, 1), :]
+        targets_ref[t, 3:4, :] = areas[pl.ds(cluster, 1), :]
     for s in range(32):
         first, second = back[(s >> 1) & 3], back[s >> 3]
         on_x = (x + jnp.where(core == 0, first, second)) & 3
         on_y = (y + jnp.where(core == 0, second, first)) & 3
         cluster = z * 32 + ((s + core) & 1) * 16 + on_y * SIDE + on_x
         for i in range(3):
-            columns[s, i : i + 1, :] = half(positions_ref[i, pl.ds(cluster, 1), :])
-        columns[s, 3:4, :] = half(areas_ref[pl.ds(cluster, 1), :])
+            columns[s, i : i + 1, :] = half(positions[i, pl.ds(cluster, 1), :])
+        columns[s, 3:4, :] = half(areas[pl.ds(cluster, 1), :])
     for s in range(32):
         upright = jnp.transpose(columns[s])
         for i in range(4):
             spread_ref[s, i] = jnp.broadcast_to(upright[:, i : i + 1], (HALF, LOADS))
-    iota = lambda shape, dim: lax.broadcasted_iota(jnp.int32, shape, dim)
-    cells, width = 128, RANK * RANK
+    last.wait()
+
+
+def make_points(here, positions, areas, couplings):
+    return pl.pallas_call(
+        points_kernel,
+        out_shape=(
+            jax.ShapeDtypeStruct((32, 4, HALF, LOADS), f32),
+            jax.ShapeDtypeStruct((8, 8, CS), f32),
+            jax.ShapeDtypeStruct(couplings.shape, bf16),
+        ),
+        in_specs=[pl.BlockSpec(memory_space=pltpu.SMEM)] + [pl.BlockSpec(memory_space=pltpu.HBM)] * 3,
+        out_specs=tuple(whole(3)),
+        scratch_shapes=[
+            pltpu.VMEM((32, 8, HALF), f32),
+            pltpu.VMEM(positions.shape, f32),
+            pltpu.VMEM(areas.shape, f32),
+            pltpu.SemaphoreType.DMA((3,)),
+        ],
+        compiler_params=pltpu.CompilerParams(vmem_limit_bytes=VMEM_LIMIT),
+        name="points",
+    )(here, in_hbm(positions), in_hbm(areas), in_hbm(couplings))
+
+
+def blocks_kernel(forward_ref, backward_ref, couplings_ref, flip_ref, blocks_ref):
+    cells = 128
     far = couplings_ref.shape[0]
 
     def summed(cell_ref):
         marks = iota((cells, far), 0) == cell_ref[...]
         return dot32(jnp.where(marks, 1.0, 0.0).astype(bf16), couplings_ref[...])
 
-    at, to = iota((width, width), 0), iota((width, width), 1)
-    flip = jnp.where((at // RANK == to % RANK) & (at % RANK == to // RANK), 1.0, 0.0)
-    total = summed(forward_ref) + dot32(summed(backward_ref).astype(bf16), flip.astype(bf16))
+    total = summed(forward_ref) + dot32(summed(backward_ref).astype(bf16), flip_ref[...])
     total = total.astype(bf16)
     columns = 16 * RANK
     row, lane = iota((cells, columns), 0), iota((cells, columns), 1)
-    same_unit = row % 16 == lane // RANK
-    spread = [
-        jnp.where(row == lane % RANK + RANK * k, 1.0, 0.0).astype(bf16) for k in range(4)
-    ]
+    same_unit = (row & 15) == (lane >> 5)
+    spread = [jnp.where(row == (lane & 31) + RANK * k, 1.0, 0.0).astype(bf16) for k in range(4)]
     place, cell = iota((16, 2 * cells), 0), iota((16, 2 * cells), 1)
-    gather = jnp.where(place == cell // 16, 1.0, 0.0).astype(bf16)
+    gather = jnp.where(place == (cell >> 4), 1.0, 0.0).astype(bf16)
     for pair in range(RANK // 2):
         parts = []
         for r in (2 * pair, 2 * pair + 1):
@@ -156,20 +217,15 @@
         blocks_ref[pair * 16 : (pair + 1) * 16] = dot32(gather, both).astype(bf16)
 
 
-def make_tables(here, forward, backward, couplings, positions, areas):
+def make_blocks(forward, backward, couplings, flip):
     return pl.pallas_call(
-        tables_kernel,
-        out_shape=(
-            jax.ShapeDtypeStruct((8 * RANK, 16 * RANK), bf16),
-            jax.ShapeDtypeStruct((32, 4, HALF, LOADS), f32),
-            jax.ShapeDtypeStruct((8, 8, CS), f32),
-        ),
-        in_specs=[pl.BlockSpec(memory_space=pltpu.SMEM)] + whole(5),
-        out_specs=tuple(whole(3)),
-        scratch_shapes=[pltpu.VMEM((32, 8, HALF), f32)],
+        blocks_kernel,
+        out_shape=jax.ShapeDtypeStruct((8 * RANK, 16 * RANK), bf16),
+        in_specs=whole(4),
+        out_specs=whole(1)[0],
         compiler_params=pltpu.CompilerParams(vmem_limit_bytes=VMEM_LIMIT),
-        name="tables",
-    )(here, forward[None, :], backward[None, :], couplings, positions, areas)
+        name="coupling_blocks",
+    )(forward[None, :], backward[None, :], couplings, flip)
 
 
 def near_kernel(first_unit, buffers, is_first, is_last, counts, targets, spread, blocks, *refs):
@@ -183,13 +239,10 @@
         keep, send, acc, refs = refs[0], refs[1], refs[2], refs[3:]
     else:
         acc, refs = refs[0], refs[1:]
-    flat, tile_a, tile_b, far, entry, sems = refs
-
-    copies = []
+    flat, tile_a, tile_b, far, entry = refs
+
     for k in range(buffers):
-        place = flat.at[k * 2 * UNIT : (k + 1) * 2 * UNIT]
-        copies.append(pltpu.make_async_copy(held[k], place, sems.at[k]))
-        copies[-1].start()
+        flat[k * 2 * UNIT : (k + 1) * 2 * UNIT] = held[k][...]
 
     def list_target(t, filled):
         for value in [counts[t, 2 * first_unit + s] for s in range(slots)]:
@@ -205,8 +258,6 @@
         acc[:, : 3 * CS] = jnp.zeros((8, 3 * CS, LOADS), f32)
     else:
         acc[...] = carried[...]
-    for copy in copies:
-        copy.wait()
 
     moments = jnp.concatenate(
         [flat[u * UNIT + 2 * DENS : (u + 1) * UNIT, :] for u in range(units)], axis=0
@@ -291,6 +342,12 @@
     count = len(buffers)
     slots = 4 * count
     is_first = carried is None
+    operands = [counts, targets, spread, blocks] + list(buffers)
+    specs = [pl.BlockSpec(memory_space=pltpu.SMEM)] + whole(3)
+    specs += whole(count)
+    if not is_first:
+        operands.append(carried)
+        specs += whole(1)
     if is_last:
         shapes = (
             jax.ShapeDtypeStruct((4, FULL, LOADS), f32),
@@ -300,12 +357,6 @@
     else:
         shapes = jax.ShapeDtypeStruct((8, FULL, LOADS), f32)
         out_specs = whole(1)[0]
-    operands = [counts, targets, spread, blocks] + list(buffers)
-    specs = [pl.BlockSpec(memory_space=pltpu.SMEM)] + whole(3)
-    specs += [pl.BlockSpec(memory_space=pl.ANY)] * count
-    if not is_first:
-        operands.append(carried)
-        specs += whole(1)
     return pl.pallas_call(
         functools.partial(near_kernel, first_unit, count, is_first, is_last),
         out_shape=shapes,
@@ -318,11 +369,11 @@
             pltpu.VMEM((6, CS, CS), bf16),
             pltpu.VMEM((8 * RANK, LOADS), f32),
             pltpu.SMEM((8 * slots + 16,), jnp.int32),
-            pltpu.SemaphoreType.DMA((count,)),
         ],
         compiler_params=pltpu.CompilerParams(vmem_limit_bytes=VMEM_LIMIT),
         cost_estimate=pl.CostEstimate(
-            flops=count * 1_000_000_000, bytes_accessed=8_000_000, transcendentals=count * 500_000
+            flops=count * 1_000_000_000, bytes_accessed=8_000_000,
+            transcendentals=count * 500_000,
         ),
         name=f"near_from_{first_unit}",
     )(*operands)
@@ -356,11 +407,9 @@
     return pl.pallas_call(
         finish_kernel,
         out_shape=jax.ShapeDtypeStruct((1, 3, CS, LOADS), bf16),
-        in_specs=[pl.BlockSpec((1, FULL, LOADS), lambda i: (0, 0, 0))] * 2
-        + [pl.BlockSpec((FULL, LOADS), lambda i: (0, 0))] * 3
-        + [pl.BlockSpec((1, 3, RANK, CS), lambda i: (0, 0, 0, 0))],
-        out_specs=pl.BlockSpec((1, 3, CS, LOADS), lambda i: (0, 0, 0, 0)),
-        grid=(1,),
+        in_specs=whole(6),
+        out_specs=whole(1)[0],
+        compiler_params=pltpu.CompilerParams(vmem_limit_bytes=VMEM_LIMIT),
         name="sum_and_expand",
     )(keep, swapped, *others, bases)
 
@@ -394,14 +443,26 @@
     positions = jnp.transpose(positions, (1, 0, 2))
 
     partner = swap_core(densities)
-    moments = moments_of(densities, bases)
-    unit = make_unit(core, densities, partner, moments)
+    own, moments, flip = moments_of(core, densities, bases)
+    unit = make_unit(core, own, partner, moments)
     from_below = along_first(unit, 1)
     from_above = along_first(unit, -1)
     from_across = along_first(unit, 2)
-    near_pairs, far_pairs, couplings, positions, areas, unit = lax.optimization_barrier(
-        (near_pairs, far_pairs, couplings, positions, areas, unit)
+    here = jnp.stack([z, core, y, x]).astype(jnp.int32)
+    here, unit = lax.optimization_barrier((here, unit))
+    spread, targets, couplings = make_points(here, positions, areas, couplings)
+    (near_pairs, far_pairs, couplings, spread, targets, unit, from_below, from_above, from_across) = (
+        lax.optimization_barrier(
+            (near_pairs, far_pairs, couplings, spread, targets, unit)
+            + (from_below, from_above, from_across)
+        )
     )
+    low = jnp.concatenate([unit, from_below], axis=0)
+    high = jnp.concatenate([from_above, from_across], axis=0)
+    low_below = along_second(low, 1)
+    high_above = along_second(high, -1)
+    high_below = along_second(high, 1)
+    low_above = along_second(low, -1)
 
     heads, tails = near_pairs[:, 0], near_pairs[:, 1]
     mark = lambda index, size: index[None, :] == jnp.arange(size, dtype=jnp.int32)[:, None]
@@ -424,30 +485,19 @@
         return jnp.where(ours, target_of(target) * 16 + unit_of(source), -1)
 
     back_cell = jnp.where(far_heads != far_tails, cell(far_tails, far_heads), -1)
-    here = jnp.stack([z, core, y, x]).astype(jnp.int32)
-    blocks, spread, targets = make_tables(
-        here, cell(far_heads, far_tails), back_cell, couplings, positions, areas
-    )
-
-    (counts, targets, spread, blocks, unit, from_below, from_above, from_across) = (
-        lax.optimization_barrier(
-            (counts, targets, spread, blocks, unit, from_below, from_above, from_across)
-        )
-    )
+    blocks = make_blocks(cell(far_heads, far_tails), back_cell, couplings, flip)
     tables = (counts, targets, spread)
-    low = jnp.concatenate([unit, from_below], axis=0)
-    high = jnp.concatenate([from_above, from_across], axis=0)
-    low_below = along_second(low, 1)
-    high_above = along_second(high, -1)
-    high_below = along_second(high, 1)
-    low_above = along_second(low, -1)
+
+    part = lambda a, b: blocks[:, a * RANK : b * RANK]
+    acc = near(0, (low, high), None, False, *tables, part(0, 4))
+    low_below, high_above, acc = lax.optimization_barrier((low_below, high_above, acc))
     low_across = along_second(low_below, 1)
     high_across = along_second(high_above, -1)
-
-    part = lambda a, b: blocks[:, a * RANK : b * RANK]
-    acc = near(0, (low, high), None, False, *tables, part(0, 4))
-    acc = near(4, (low_below, high_below, low_above, high_above), acc, False, *tables, part(4, 12))
-    keep, send = near(12, (low_across, high_across), acc, True, *tables, part(12, 16))
+    acc = near(
+        4, (low_below, high_below, low_above, high_above), acc, False, *tables, part(4, 12)
+    )
+    last = (low_across, high_across)
+    keep, send = near(12, last, acc, True, *tables, part(12, 16))
 
     swapped = swap_core(send)
     both = [(keep[k] + swapped[k].astype(f32)).astype(bf16) for k in range(1, 4)]

time: 75.4 us -> 65.8 us (0.87)
  the two profiles are of different devices: /device:TPU:28 before, /device:TPU:1 now
where the time goes in v3:
time: 65.8 us; the launch traced here: 64.9 us
  Pallas kernels  29.2 us (44%)
  starting transfers between devices  20.9 us (32%)
  waiting for transfers between devices  13.7 us (21%)
    pallas_call x3, Pallas kernels, near(): pl.pallas_call(functools.partial(near_kernel, first_unit, count, is_first...  18.3 us
    ppermute x3, waiting for transfers between devices, along_z(): lax.ppermute(value, AXES, routes(lambda z, c, y, x: (z + step, c, y, x)))  10.9 us
    ppermute x6, starting transfers between devices, along_second(): return lax.ppermute(value, AXES, routes(move))  7.03 us
    ppermute x2, starting transfers between devices, swap_core(): lax.ppermute(value, AXES, routes(lambda z, c, y, x: (z, 1 - c, y, x)))  5.94 us
    pallas_call x1, Pallas kernels, make_points(): pl.pallas_call(points_kernel, out_shape=(jax.ShapeDtypeStruct((32, 4, HAL...  4.6 us
    ppermute x3, starting transfers between devices, along_first(): return lax.ppermute(value, AXES, routes(move))  4.54 us
    pallas_call x1, Pallas kernels, make_blocks(): pl.pallas_call(blocks_kernel, out_shape=jax.ShapeDtypeStruct((8 * RANK, 1...  4.15 us
    ppermute x3, starting transfers between devices, along_z(): lax.ppermute(value, AXES, routes(lambda z, c, y, x: (z + step, c, y, x)))  3.41 us
  transfers between devices with their start and end apart: 14, of which 6 were waited for; matrix products, arithmetic and copies ran while one was open for 1% of the time, Pallas kernels for 36%

profile of v3, /device:TPU:1, one launch (start us, length us, event | category | flops | bytes accessed | tf_op | source)
XLA Modules:
  0.0 64.9 jit_solution(8823950820782792441)
XLA Ops:
  0.0 1.4 %collective-permute-start = (bf16[1,3,256,128]{3,2,1,0:T(8,128)(2,1)}, bf16[1,3,256,128]{3,2,1,0:T(8,128)(2,1)S(1)}, u32[]{:S(2)}, u32[]{:S(2)}) collective-permute-start(bf16[1,3,256,128]{3,2,1,0:T(8,128)(2,1)} %dens_ref.1), channel_id=1, source_target_pairs={{0,16},{1,17},{2,18},{3,19},{4,20},{5,21},{6,22},{7,23},{8,24},{9,... | collective-permute-start | bytes 589832 | tf_op jit(solution)/shard_map/ppermute | solution.py:43
  1.4 1.1 %moments.1 = (bf16[384,128]{1,0:T(8,128)(2,1)S(1)}, bf16[32,128]{1,0:T(8,128)(2,1)S(1)}, bf16[1024,1024]{1,0:T(8,128)(2,1)S(1)}) custom-call(s32[1]{0:T(128)} %bitcast.1.core_ref, bf16[1,3,256,128]{3,2,1,0:T(8,128)(2,1)} %dens_ref.1, bf16[1,3,32,256]{3,2,1,0:T(8,128)(2,1)} %bitcast.87), custom_call_target="tpu_custom_call" | custom-call | tf_op jit(solution)/shard_map/moments/pallas_call | solution.py:102
  2.5 0.2 collective-permute-done.partner_ref
  2.7 0.0 copy-start.2
  2.7 0.0 copy-start.1
  2.7 0.1 unit.1
  2.8 3.1 %collective-permute-start.3 = (bf16[800,128]{1,0:T(8,128)(2,1)S(1)}, bf16[800,128]{1,0:T(8,128)(2,1)S(1)}, u32[]{:S(2)}, u32[]{:S(2)}) collective-permute-start(bf16[800,128]{1,0:T(8,128)(2,1)S(1)} %unit.1), channel_id=1, source_target_pairs={{0,2},{1,3},{2,0},{3,1},{4,6},{5,7},{6,4},{7,5},{8,10},{9,11},{10,... | collective-permute-start | bytes 614408 | tf_op jit(solution)/shard_map/ppermute | solution.py:48
  5.9 0.8 %collective-permute-start.2 = (bf16[800,128]{1,0:T(8,128)(2,1)S(1)}, bf16[800,128]{1,0:T(8,128)(2,1)S(1)}, u32[]{:S(2)}, u32[]{:S(2)}) collective-permute-start(bf16[800,128]{1,0:T(8,128)(2,1)S(1)} %unit.1), channel_id=1, source_target_pairs={{0,3},{1,0},{2,1},{3,2},{4,7},{5,4},{6,5},{7,6},{8,11},{9,8},{10,9... | collective-permute-start | bytes 614408 | tf_op jit(solution)/shard_map/ppermute | solution.py:48
  6.7 0.7 %collective-permute-start.1 = (bf16[800,128]{1,0:T(8,128)(2,1)S(1)}, bf16[800,128]{1,0:T(8,128)(2,1)S(1)}, u32[]{:S(2)}, u32[]{:S(2)}) collective-permute-start(bf16[800,128]{1,0:T(8,128)(2,1)S(1)} %unit.1), channel_id=1, source_target_pairs={{0,1},{1,2},{2,3},{3,0},{4,5},{5,6},{6,7},{7,4},{8,9},{9,10},{10,1... | collective-permute-start | bytes 614408 | tf_op jit(solution)/shard_map/ppermute | solution.py:48
  7.3 0.1 pad_add_fusion.2.here_ref
  7.4 4.6 %points.1 = (f32[32,4,128,128]{3,2,1,0:T(8,128)S(1)}, f32[8,8,256]{2,1,0:T(8,128)S(1)}, bf16[768,1024]{1,0:T(8,128)(2,1)S(1)}) custom-call(s32[4]{0:T(128)S(1)} %pad_add_fusion.2.here_ref, f32[3,128,256]{2,1,0:T(8,128)} %bitcast.89, f32[128,256]{1,0:T(8,128)} %areas_ref.1, bf16[768,1024]{1,0:T(8,128)(2,1)} %couplings_ref.1), custom_call_target="tpu_custom_call" | custom-call | tf_op jit(solution)/shard_map/points/pallas_call | solution.py:174
  12.0 0.0 collective-permute-done.3
  12.0 0.0 collective-permute-done.2
  12.1 0.7 %collective-permute-done.1 = bf16[800,128]{1,0:T(8,128)(2,1)S(1)} collective-permute-done((bf16[800,128]{1,0:T(8,128)(2,1)S(1)}, bf16[800,128]{1,0:T(8,128)(2,1)S(1)}, u32[]{:S(2)}, u32[]{:S(2)}) %collective-permute-start.1) | collective-permute-done | bytes 204832 | tf_op jit(solution)/shard_map/ppermute | solution.py:48
  12.8 1.0 %collective-permute-start.8 = (bf16[1600,128]{1,0:T(8,128)(2,1)S(1)}, bf16[1600,128]{1,0:T(8,128)(2,1)S(1)}, u32[]{:S(2)}, u32[]{:S(2)}) collective-permute-start(bf16[1600,128]{1,0:T(8,128)(2,1)S(1)} %constant_dynamic-update-slice_fusion.2.refs_1_), channel_id=1, source_target_pairs={{0,4},{1,5},{2,6},{3,7},{4,8},{5,9},{6,10},{7,11},{8,12},{9,13},{1... | collective-permute-start | bytes 1228808 | tf_op jit(solution)/shard_map/ppermute | solution.py:53
  13.8 1.8 %collective-permute-start.5 = (bf16[1600,128]{1,0:T(8,128)(2,1)S(1)}, bf16[1600,128]{1,0:T(8,128)(2,1)S(1)}, u32[]{:S(2)}, u32[]{:S(2)}) collective-permute-start(bf16[1600,128]{1,0:T(8,128)(2,1)S(1)} %constant_dynamic-update-slice_fusion.2.refs_1_), channel_id=1, source_target_pairs={{0,12},{1,13},{2,14},{3,15},{4,0},{5,1},{6,2},{7,3},{8,4},{9,5},{1... | collective-permute-start | bytes 1228808 | tf_op jit(solution)/shard_map/ppermute | solution.py:53
  15.6 1.0 %collective-permute-start.9 = (bf16[1600,128]{1,0:T(8,128)(2,1)S(1)}, bf16[1600,128]{1,0:T(8,128)(2,1)S(1)}, u32[]{:S(2)}, u32[]{:S(2)}) collective-permute-start(bf16[1600,128]{1,0:T(8,128)(2,1)S(1)} %constant_dynamic-update-slice_fusion.refs_0_), channel_id=1, source_target_pairs={{0,12},{1,13},{2,14},{3,15},{4,0},{5,1},{6,2},{7,3},{8,4},{9,5},{1... | collective-permute-start | bytes 1228808 | tf_op jit(solution)/shard_map/ppermute | solution.py:53
  16.7 0.5 collective-permute-start.4
  17.2 0.0 copy-done.2
  17.2 0.1 bitcast_select_fusion.2
  17.2 0.0 copy-done.1
  17.3 0.2 fusion.16
  17.5 4.2 %coupling_blocks.1 = bf16[256,512]{1,0:T(8,128)(2,1)S(1)} custom-call(s32[1,768]{1,0:T(1,128)S(1)} %get-tuple-element.59.forward_ref, s32[1,768]{1,0:T(1,128)S(1)} %get-tuple-element.58.backward_ref, bf16[768,1024]{1,0:T(8,128)(2,1)S(1)} %get-tuple-element.38.couplings_ref, bf16[1024,1024]{1,0:T(8,128)(2,1)S(1)} %get-tuple-element.39.flip_ref), custom_call_target="tpu_custom_call" | custom-call | tf_op jit(solution)/shard_map/coupling_blocks/pallas_call | solution.py:221
  21.7 0.2 fusion.2.counts
  21.9 4.6 %near_from_0.1.refs_4_ = f32[8,800,128]{2,1,0:T(8,128)S(1)} custom-call(s32[8,32]{1,0:T(8,128)S(1)} %fusion.2.counts, f32[8,8,256]{2,1,0:T(8,128)S(1)} %get-tuple-element.35.targets, f32[32,4,128,128]{3,2,1,0:T(8,128)S(1)} %get-tuple-element.36.spread, bf16[256,128]{1,0:T(8,128)(2,1)S(1)} %get-tuple-element.56.blocks, ...), custom_call_target="tpu_custom_call" | custom-call | flops 2000000000 | bytes 8000000 | tf_op jit(solution)/shard_map/near_from_0/pallas_call | solution.py:360
  26.5 0.0 collective-permute-done.5.refs_3_
  26.5 0.0 collective-permute-done.4.refs_0_
  26.5 0.1 collective-permute-start.6
  26.6 2.7 %collective-permute-start.7 = (bf16[1600,128]{1,0:T(8,128)(2,1)S(1)}, bf16[1600,128]{1,0:T(8,128)(2,1)S(1)}, u32[]{:S(2)}, u32[]{:S(2)}) collective-permute-start(bf16[1600,128]{1,0:T(8,128)(2,1)S(1)} %collective-permute-done.5.refs_3_), channel_id=1, source_target_pairs={{0,12},{1,13},{2,14},{3,15},{4,0},{5,1},{6,2},{7,3},{8,4},{9,5},{1... | collective-permute-start | bytes 1228808 | tf_op jit(solution)/shard_map/ppermute | solution.py:53
  29.3 0.0 collective-permute-done.8.refs_1_
  29.3 0.0 collective-permute-done.9.refs_2_
  29.3 8.8 %near_from_4.1.refs_2_ = f32[8,800,128]{2,1,0:T(8,128)S(1)} custom-call(s32[8,32]{1,0:T(8,128)S(1)} %fusion.2.counts, f32[8,8,256]{2,1,0:T(8,128)S(1)} %get-tuple-element.35.targets, f32[32,4,128,128]{3,2,1,0:T(8,128)S(1)} %get-tuple-element.36.spread, bf16[256,256]{1,0:T(8,128)(2,1)S(1)} %slice.54.blocks, ...), custom_call_target="tpu_custom_call" | custom-call | flops 4000000000 | bytes 8000000 | tf_op jit(solution)/shard_map/near_from_4/pallas_call | solution.py:360
  38.1 0.0 collective-permute-done.6.refs_0_
  38.2 0.0 collective-permute-done.7.refs_1_
  38.2 4.9 %near_from_12.1 = (f32[4,800,128]{2,1,0:T(8,128)S(1)}, bf16[4,800,128]{2,1,0:T(8,128)(2,1)S(1)}) custom-call(s32[8,32]{1,0:T(8,128)S(1)} %fusion.2.counts, f32[8,8,256]{2,1,0:T(8,128)S(1)} %get-tuple-element.35.targets, f32[32,4,128,128]{3,2,1,0:T(8,128)S(1)} %get-tuple-element.36.spread, bf16[256,128]{1,0:T(8,128)(2,1)S(1)} %get-tuple-element.57.blocks, ...), custom_call_target="tpu_custom_call" | custom-call | flops 2000000000 | bytes 8000000 | tf_op jit(solution)/shard_map/near_from_12/pallas_call | solution.py:360
  43.1 0.0 copy-start
  43.1 4.5 %collective-permute-start.10 = (bf16[4,800,128]{2,1,0:T(8,128)(2,1)S(1)}, bf16[4,800,128]{2,1,0:T(8,128)(2,1)S(1)}, u32[]{:S(2)}, u32[]{:S(2)}) collective-permute-start(bf16[4,800,128]{2,1,0:T(8,128)(2,1)S(1)} %get-tuple-element.48), channel_id=1, source_target_pairs={{0,16},{1,17},{2,18},{3,19},{4,20},{5,21},{6,22},{7,23},{8,24},{9,... | collective-permute-start | bytes 2457608 | tf_op jit(solution)/shard_map/ppermute | solution.py:43
  47.6 2.0 %collective-permute-done.10.swapped = bf16[4,800,128]{2,1,0:T(8,128)(2,1)S(1)} collective-permute-done((bf16[4,800,128]{2,1,0:T(8,128)(2,1)S(1)}, bf16[4,800,128]{2,1,0:T(8,128)(2,1)S(1)}, u32[]{:S(2)}, u32[]{:S(2)}) %collective-permute-start.10) | collective-permute-done | bytes 819232 | tf_op jit(solution)/shard_map/ppermute | solution.py:43
  49.6 0.1 fusion.6
  49.7 1.4 %collective-permute-start.13 = (bf16[800,128]{1,0:T(8,128)(2,1)S(1)}, bf16[800,128]{1,0:T(8,128)(2,1)S(1)}, u32[]{:S(2)}, u32[]{:S(2)}) collective-permute-start(bf16[800,128]{1,0:T(8,128)(2,1)S(1)} %get-tuple-element.53), channel_id=1, source_target_pairs={{0,96},{1,97},{2,98},{3,99},{4,100},{5,101},{6,102},{7,103},{8,104... | collective-permute-start | bytes 614408 | tf_op jit(solution)/shard_map/ppermute | solution.py:57
  51.1 1.4 %collective-permute-start.12 = (bf16[800,128]{1,0:T(8,128)(2,1)S(1)}, bf16[800,128]{1,0:T(8,128)(2,1)S(1)}, u32[]{:S(2)}, u32[]{:S(2)}) collective-permute-start(bf16[800,128]{1,0:T(8,128)(2,1)S(1)} %get-tuple-element.54), channel_id=1, source_target_pairs={{0,64},{1,65},{2,66},{3,67},{4,68},{5,69},{6,70},{7,71},{8,72},{9,... | collective-permute-start | bytes 614408 | tf_op jit(solution)/shard_map/ppermute | solution.py:57
  52.5 0.6 collective-permute-start.11
  53.1 2.9 %collective-permute-done.13.three = bf16[800,128]{1,0:T(8,128)(2,1)S(1)} collective-permute-done((bf16[800,128]{1,0:T(8,128)(2,1)S(1)}, bf16[800,128]{1,0:T(8,128)(2,1)S(1)}, u32[]{:S(2)}, u32[]{:S(2)}) %collective-permute-start.13) | collective-permute-done | bytes 204832 | tf_op jit(solution)/shard_map/ppermute | solution.py:57
  56.1 2.5 %collective-permute-done.12.two = bf16[800,128]{1,0:T(8,128)(2,1)S(1)} collective-permute-done((bf16[800,128]{1,0:T(8,128)(2,1)S(1)}, bf16[800,128]{1,0:T(8,128)(2,1)S(1)}, u32[]{:S(2)}, u32[]{:S(2)}) %collective-permute-start.12) | collective-permute-done | bytes 204832 | tf_op jit(solution)/shard_map/ppermute | solution.py:57
  58.6 5.4 %collective-permute-done.11.one = bf16[800,128]{1,0:T(8,128)(2,1)S(1)} collective-permute-done((bf16[800,128]{1,0:T(8,128)(2,1)S(1)}, bf16[800,128]{1,0:T(8,128)(2,1)S(1)}, u32[]{:S(2)}, u32[]{:S(2)}) %collective-permute-start.11) | collective-permute-done | bytes 204832 | tf_op jit(solution)/shard_map/ppermute | solution.py:57
  64.0 0.0 copy-done
  64.0 0.9 %sum_and_expand.1 = bf16[1,3,256,128]{3,2,1,0:T(8,128)(2,1)} custom-call(f32[4,800,128]{2,1,0:T(8,128)S(1)} %get-tuple-element.47.keep, bf16[4,800,128]{2,1,0:T(8,128)(2,1)S(1)} %collective-permute-done.10.swapped, bf16[800,128]{1,0:T(8,128)(2,1)S(1)} %collective-permute-done.11.one, bf16[800,128]{1,0:T(8,128)(2,1)S(1)} %collective-permute-done.12.two, ...), custom_call_target="tpu_custom_call" | custom-call | tf_op jit(solution)/shard_map/sum_and_expand/pallas_call | solution.py:407
  (8 shorter events, 0.1 us)
Async XLA Ops:
  0.0 2.7 %collective-permute-start = (bf16[1,3,256,128]{3,2,1,0:T(8,128)(2,1)}, bf16[1,3,256,128]{3,2,1,0:T(8,128)(2,1)S(1)}, u32[]{:S(2)}, u32[]{:S(2)}) collective-permute-start(bf16[1,3,256,128]{3,2,1,0:T(8,128)(2,1)} %dens_ref.1), channel_id=1, source_target_pairs={{0,16},{1,17},{2,18},{3,19},{4,20},{5,21},{6,22},{7,23},{8,24},{9,... | collective-permute-start | bytes 589832 | tf_op jit(solution)/shard_map/ppermute | solution.py:43
  2.7 14.5 %copy-start.2 = (s32[768,2]{0,1:T(2,128)S(1)}, s32[768,2]{0,1:T(2,128)}, u32[]{:S(2)}) copy-start(s32[768,2]{0,1:T(2,128)} %param.12) | copy-start | bytes 18436
  2.7 14.5 %copy-start.1 = (s32[1920,2]{0,1:T(2,128)S(1)}, s32[1920,2]{0,1:T(2,128)}, u32[]{:S(2)}) copy-start(s32[1920,2]{0,1:T(2,128)} %param.11) | copy-start | bytes 46084
  2.8 9.2 %collective-permute-start.3 = (bf16[800,128]{1,0:T(8,128)(2,1)S(1)}, bf16[800,128]{1,0:T(8,128)(2,1)S(1)}, u32[]{:S(2)}, u32[]{:S(2)}) collective-permute-start(bf16[800,128]{1,0:T(8,128)(2,1)S(1)} %unit.1), channel_id=1, source_target_pairs={{0,2},{1,3},{2,0},{3,1},{4,6},{5,7},{6,4},{7,5},{8,10},{9,11},{10,... | collective-permute-start | bytes 614408 | tf_op jit(solution)/shard_map/ppermute | solution.py:48
  5.9 6.2 %collective-permute-start.2 = (bf16[800,128]{1,0:T(8,128)(2,1)S(1)}, bf16[800,128]{1,0:T(8,128)(2,1)S(1)}, u32[]{:S(2)}, u32[]{:S(2)}) collective-permute-start(bf16[800,128]{1,0:T(8,128)(2,1)S(1)} %unit.1), channel_id=1, source_target_pairs={{0,3},{1,0},{2,1},{3,2},{4,7},{5,4},{6,5},{7,6},{8,11},{9,8},{10,9... | collective-permute-start | bytes 614408 | tf_op jit(solution)/shard_map/ppermute | solution.py:48
  6.7 6.1 %collective-permute-start.1 = (bf16[800,128]{1,0:T(8,128)(2,1)S(1)}, bf16[800,128]{1,0:T(8,128)(2,1)S(1)}, u32[]{:S(2)}, u32[]{:S(2)}) collective-permute-start(bf16[800,128]{1,0:T(8,128)(2,1)S(1)} %unit.1), channel_id=1, source_target_pairs={{0,1},{1,2},{2,3},{3,0},{4,5},{5,6},{6,7},{7,4},{8,9},{9,10},{10,1... | collective-permute-start | bytes 614408 | tf_op jit(solution)/shard_map/ppermute | solution.py:48
  12.8 16.5 %collective-permute-start.8 = (bf16[1600,128]{1,0:T(8,128)(2,1)S(1)}, bf16[1600,128]{1,0:T(8,128)(2,1)S(1)}, u32[]{:S(2)}, u32[]{:S(2)}) collective-permute-start(bf16[1600,128]{1,0:T(8,128)(2,1)S(1)} %constant_dynamic-update-slice_fusion.2.refs_1_), channel_id=1, source_target_pairs={{0,4},{1,5},{2,6},{3,7},{4,8},{5,9},{6,10},{7,11},{8,12},{9,13},{1... | collective-permute-start | bytes 1228808 | tf_op jit(solution)/shard_map/ppermute | solution.py:53
  13.8 12.7 %collective-permute-start.5 = (bf16[1600,128]{1,0:T(8,128)(2,1)S(1)}, bf16[1600,128]{1,0:T(8,128)(2,1)S(1)}, u32[]{:S(2)}, u32[]{:S(2)}) collective-permute-start(bf16[1600,128]{1,0:T(8,128)(2,1)S(1)} %constant_dynamic-update-slice_fusion.2.refs_1_), channel_id=1, source_target_pairs={{0,12},{1,13},{2,14},{3,15},{4,0},{5,1},{6,2},{7,3},{8,4},{9,5},{1... | collective-permute-start | bytes 1228808 | tf_op jit(solution)/shard_map/ppermute | solution.py:53
  15.6 13.7 %collective-permute-start.9 = (bf16[1600,128]{1,0:T(8,128)(2,1)S(1)}, bf16[1600,128]{1,0:T(8,128)(2,1)S(1)}, u32[]{:S(2)}, u32[]{:S(2)}) collective-permute-start(bf16[1600,128]{1,0:T(8,128)(2,1)S(1)} %constant_dynamic-update-slice_fusion.refs_0_), channel_id=1, source_target_pairs={{0,12},{1,13},{2,14},{3,15},{4,0},{5,1},{6,2},{7,3},{8,4},{9,5},{1... | collective-permute-start | bytes 1228808 | tf_op jit(solution)/shard_map/ppermute | solution.py:53
  16.7 9.9 %collective-permute-start.4 = (bf16[1600,128]{1,0:T(8,128)(2,1)S(1)}, bf16[1600,128]{1,0:T(8,128)(2,1)S(1)}, u32[]{:S(2)}, u32[]{:S(2)}) collective-permute-start(bf16[1600,128]{1,0:T(8,128)(2,1)S(1)} %constant_dynamic-update-slice_fusion.refs_0_), channel_id=1, source_target_pairs={{0,4},{1,5},{2,6},{3,7},{4,8},{5,9},{6,10},{7,11},{8,12},{9,13},{1... | collective-permute-start | bytes 1228808 | tf_op jit(solution)/shard_map/ppermute | solution.py:53
  26.5 11.6 %collective-permute-start.6 = (bf16[1600,128]{1,0:T(8,128)(2,1)S(1)}, bf16[1600,128]{1,0:T(8,128)(2,1)S(1)}, u32[]{:S(2)}, u32[]{:S(2)}) collective-permute-start(bf16[1600,128]{1,0:T(8,128)(2,1)S(1)} %collective-permute-done.4.refs_0_), channel_id=1, source_target_pairs={{0,4},{1,5},{2,6},{3,7},{4,8},{5,9},{6,10},{7,11},{8,12},{9,13},{1... | collective-permute-start | bytes 1228808 | tf_op jit(solution)/shard_map/ppermute | solution.py:53
  26.6 11.5 %collective-permute-start.7 = (bf16[1600,128]{1,0:T(8,128)(2,1)S(1)}, bf16[1600,128]{1,0:T(8,128)(2,1)S(1)}, u32[]{:S(2)}, u32[]{:S(2)}) collective-permute-start(bf16[1600,128]{1,0:T(8,128)(2,1)S(1)} %collective-permute-done.5.refs_3_), channel_id=1, source_target_pairs={{0,12},{1,13},{2,14},{3,15},{4,0},{5,1},{6,2},{7,3},{8,4},{9,5},{1... | collective-permute-start | bytes 1228808 | tf_op jit(solution)/shard_map/ppermute | solution.py:53
  43.1 20.9 %copy-start = (bf16[1,32,3,256]{3,1,2,0:T(8,128)(2,1)S(1)}, bf16[1,32,3,256]{3,1,2,0:T(8,128)(2,1)}, u32[]{:S(2)}) copy-start(bf16[1,32,3,256]{3,1,2,0:T(8,128)(2,1)} %param.10) | copy-start | bytes 147460
  43.1 6.5 %collective-permute-start.10 = (bf16[4,800,128]{2,1,0:T(8,128)(2,1)S(1)}, bf16[4,800,128]{2,1,0:T(8,128)(2,1)S(1)}, u32[]{:S(2)}, u32[]{:S(2)}) collective-permute-start(bf16[4,800,128]{2,1,0:T(8,128)(2,1)S(1)} %get-tuple-element.48), channel_id=1, source_target_pairs={{0,16},{1,17},{2,18},{3,19},{4,20},{5,21},{6,22},{7,23},{8,24},{9,... | collective-permute-start | bytes 2457608 | tf_op jit(solution)/shard_map/ppermute | solution.py:43
  49.7 6.4 %collective-permute-start.13 = (bf16[800,128]{1,0:T(8,128)(2,1)S(1)}, bf16[800,128]{1,0:T(8,128)(2,1)S(1)}, u32[]{:S(2)}, u32[]{:S(2)}) collective-permute-start(bf16[800,128]{1,0:T(8,128)(2,1)S(1)} %get-tuple-element.53), channel_id=1, source_target_pairs={{0,96},{1,97},{2,98},{3,99},{4,100},{5,101},{6,102},{7,103},{8,104... | collective-permute-start | bytes 614408 | tf_op jit(solution)/shard_map/ppermute | solution.py:57
  51.1 7.5 %collective-permute-start.12 = (bf16[800,128]{1,0:T(8,128)(2,1)S(1)}, bf16[800,128]{1,0:T(8,128)(2,1)S(1)}, u32[]{:S(2)}, u32[]{:S(2)}) collective-permute-start(bf16[800,128]{1,0:T(8,128)(2,1)S(1)} %get-tuple-element.54), channel_id=1, source_target_pairs={{0,64},{1,65},{2,66},{3,67},{4,68},{5,69},{6,70},{7,71},{8,72},{9,... | collective-permute-start | bytes 614408 | tf_op jit(solution)/shard_map/ppermute | solution.py:57
  52.5 11.5 %collective-permute-start.11 = (bf16[800,128]{1,0:T(8,128)(2,1)S(1)}, bf16[800,128]{1,0:T(8,128)(2,1)S(1)}, u32[]{:S(2)}, u32[]{:S(2)}) collective-permute-start(bf16[800,128]{1,0:T(8,128)(2,1)S(1)} %get-tuple-element.55), channel_id=1, source_target_pairs={{0,32},{1,33},{2,34},{3,35},{4,36},{5,37},{6,38},{7,39},{8,40},{9,... | collective-permute-start | bytes 614408 | tf_op jit(solution)/shard_map/ppermute | solution.py:57
